TPU v7x, 256 devices: a whole 4x4x8 slice. The times are simulated.
256 devices in a mesh: ctx: 64 (over y, z, core), grp: 4 (over x).
Axes of the slice: x: 4, y: 4, z: 8, core: 2. Of those that a mesh axis runs over, the one named last changes fastest.
Arguments:
- queries: bfloat16 [65536, 1024], P(('ctx', 'grp')), may hold values from -6 to 6
- key_rows: bfloat16 [65536, 128], P(('ctx', 'grp')), may hold values from -6 to 6
- value_rows: bfloat16 [65536, 128], P(('ctx', 'grp')), may hold values from -6 to 6
- out_grad: bfloat16 [65536, 1024], P(('ctx', 'grp')), may hold values from -6 to 6
- doc_lengths: int32 [128], replicated, may hold values from 1 to 1024, 65536 in all
Outputs:
- attended: bfloat16 [65536, 1024], P(('ctx', 'grp'))
- query_grad: bfloat16 [65536, 1024], P(('ctx', 'grp'))
- key_grad: bfloat16 [65536, 128], P(('ctx', 'grp'))
- value_grad: bfloat16 [65536, 128], P(('ctx', 'grp'))
Inputs may be any that keep to these rules, and one draw needn't show every extreme that they name: `doc_lengths`: the lengths sum to 65536; one document has exactly 1024 tokens.
All inputs are finite; a program needn't handle non-finite values.
Results may differ from a plain program's by a relative error of at most 0.028.
Values may be sent and summed in bfloat16 or wider, within the bound.
No kernel may reach another device: no remote copies, remote signals or barrier semaphores. Data moves between devices by JAX's collectives and lax.ppermute only.
A program may use at most 64 MiB of HBM per device.

v0:
```python
import math

import jax
import jax.numpy as jnp
from jax import lax
from jax.sharding import PartitionSpec as P

REACH = 4


def passed_along(block, axis, distance):
    devices = range(lax.axis_size(axis))
    route = [(i - distance, i) for i in devices if i - distance in devices]
    return lax.ppermute(block, axis, route)


def window_attention(query_part, window, grad_part, query_first, key_first, doc_start):
    row_count = query_part.shape[0]
    width = window.shape[0]
    head_dim = window.shape[1] // 2
    heads = query_part.shape[1] // head_dim
    keys_win = window[:, :head_dim]
    values_win = window[:, head_dim:]
    factor = 1.0 / math.sqrt(head_dim)
    step_rows = min(128, row_count)
    key_pos = key_first + jnp.arange(width, dtype=jnp.int32)
    grad_window = jnp.zeros((width, 2 * head_dim), jnp.float32)
    outputs = []
    qgrads = []
    for block_index in range(row_count // step_rows):
        low = block_index * step_rows
        query_pos = query_first + low + jnp.arange(step_rows, dtype=jnp.int32)
        begins = jnp.max(
            jnp.where(doc_start[None, :] <= query_pos[:, None], doc_start[None, :], 0), axis=1
        )
        visible = (key_pos[None, :] >= begins[:, None]) & (key_pos[None, :] <= query_pos[:, None])
        mask_three = visible[:, None, :]
        query_flat = query_part[low : low + step_rows].reshape(step_rows * heads, head_dim)
        grad_flat = grad_part[low : low + step_rows].reshape(step_rows * heads, head_dim)
        scores = lax.dot_general(
            query_flat, keys_win, (((1,), (1,)), ((), ())), preferred_element_type=jnp.float32
        )
        scores = scores.reshape(step_rows, heads, width) * factor
        highest = jnp.max(jnp.where(mask_three, scores, -jnp.inf), axis=2, keepdims=True)
        weights = jnp.exp(jnp.where(mask_three, scores - highest, -jnp.inf))
        denom = jnp.sum(weights, axis=2, keepdims=True)
        probs = (weights / denom).reshape(step_rows * heads, width)
        probs_low = probs.astype(jnp.bfloat16)
        output_low = jnp.dot(probs_low, values_win, preferred_element_type=jnp.float32).astype(
            jnp.bfloat16
        )
        dprobs = lax.dot_general(
            grad_flat, values_win, (((1,), (1,)), ((), ())), preferred_element_type=jnp.float32
        )
        deltas = jnp.sum(
            grad_flat.astype(jnp.float32) * output_low.astype(jnp.float32), axis=1, keepdims=True
        )
        dscores = (probs * (dprobs - deltas) * factor).astype(jnp.bfloat16)
        qgrad_low = jnp.dot(dscores, keys_win, preferred_element_type=jnp.float32).astype(
            jnp.bfloat16
        )
        key_part = lax.dot_general(
            dscores, query_flat, (((0,), (0,)), ((), ())), preferred_element_type=jnp.float32
        )
        value_part = lax.dot_general(
            probs_low, grad_flat, (((0,), (0,)), ((), ())), preferred_element_type=jnp.float32
        )
        grad_window = grad_window + jnp.concatenate([key_part, value_part], axis=1)
        outputs.append(output_low.reshape(step_rows, heads * head_dim))
        qgrads.append(qgrad_low.reshape(step_rows, heads * head_dim))
    return (jnp.concatenate(outputs, axis=0), jnp.concatenate(qgrads, axis=0), grad_window)


def starts_of(doc_lengths):
    return jnp.cumsum(doc_lengths) - doc_lengths


def body(queries, key_rows, value_rows, out_grad, doc_lengths):
    row_count = queries.shape[0]
    head_dim = key_rows.shape[1]
    offset = lax.axis_index(("ctx", "grp")) * row_count
    doc_start = starts_of(doc_lengths)
    packed = jnp.concatenate([key_rows, value_rows], axis=1)
    pieces = []
    for distance in range(REACH, 0, -1):
        pieces.append(passed_along(packed, ("ctx", "grp"), distance))
    pieces.append(packed)
    window = jnp.concatenate(pieces, axis=0)
    attended, query_grad, grad_window = window_attention(
        queries, window, out_grad, offset, offset - REACH * row_count, doc_start
    )
    mine = grad_window[REACH * row_count :]
    for distance in range(1, REACH + 1):
        lower = (REACH - distance) * row_count
        mine = mine + passed_along(
            grad_window[lower : lower + row_count], ("ctx", "grp"), -distance
        )
    return (
        attended,
        query_grad,
        mine[:, :head_dim].astype(jnp.bfloat16),
        mine[:, head_dim:].astype(jnp.bfloat16),
    )


def solution(mesh):
    in_specs = (
        P(("ctx", "grp"), None),
        P(("ctx", "grp"), None),
        P(("ctx", "grp"), None),
        P(("ctx", "grp"), None),
        P(),
    )
    out_specs = (
        P(("ctx", "grp"), None),
        P(("ctx", "grp"), None),
        P(("ctx", "grp"), None),
        P(("ctx", "grp"), None),
    )
    return jax.shard_map(body, mesh=mesh, in_specs=in_specs, out_specs=out_specs, check_vma=False)
```

profile of v0, /device:TPU:16, one launch (start us, length us, event | category | flops | bytes accessed | tf_op | source)
XLA Modules:
  0.0 84.6 jit_solution(13677370274811708301)
XLA Ops:
  0.6 1.5 %constant_dynamic-update-slice_fusion.1 = bf16[256,256]{1,0:T(8,128)(2,1)} fusion(bf16[256,128]{1,0:T(8,128)(2,1)} %param.6), kind=kLoop, calls=%fused_computation.59 | loop fusion | bytes 131072
  2.1 1.5 %constant_dynamic-update-slice_fusion = bf16[256,256]{1,0:T(8,128)(2,1)} fusion(bf16[256,256]{1,0:T(8,128)(2,1)} %constant_dynamic-update-slice_fusion.1, bf16[256,128]{1,0:T(8,128)(2,1)} %param.7), kind=kLoop, calls=%fused_computation.58 | loop fusion | bytes 131072 | tf_op jit(solution)/shard_map/concatenate | solution.py:83
  3.6 3.4 %collective-permute-start.3 = (bf16[256,256]{1,0:T(8,128)(2,1)}, bf16[256,256]{1,0:T(8,128)(2,1)}, u32[]{:S(2)}, u32[]{:S(2)}) collective-permute-start(bf16[256,256]{1,0:T(8,128)(2,1)} %constant_dynamic-update-slice_fusion), channel_id=1, source_target_pairs={{0,1},{1,2},{2,3},{3,4},{4,5},{5,6},{6,7},{7,8},{8,9},{9,10},{10,1... | collective-permute-start | bytes 393224 | tf_op jit(solution)/shard_map/ppermute | solution.py:14
  7.0 4.6 %collective-permute-start.2 = (bf16[256,256]{1,0:T(8,128)(2,1)}, bf16[256,256]{1,0:T(8,128)(2,1)}, u32[]{:S(2)}, u32[]{:S(2)}) collective-permute-start(bf16[256,256]{1,0:T(8,128)(2,1)} %constant_dynamic-update-slice_fusion), channel_id=1, source_target_pairs={{0,2},{1,3},{2,4},{3,5},{4,6},{5,7},{6,8},{7,9},{8,10},{9,11},{10,... | collective-permute-start | bytes 393224 | tf_op jit(solution)/shard_map/ppermute | solution.py:14
  11.6 2.5 %collective-permute-start.1 = (bf16[256,256]{1,0:T(8,128)(2,1)}, bf16[256,256]{1,0:T(8,128)(2,1)}, u32[]{:S(2)}, u32[]{:S(2)}) collective-permute-start(bf16[256,256]{1,0:T(8,128)(2,1)} %constant_dynamic-update-slice_fusion), channel_id=1, source_target_pairs={{0,3},{1,4},{2,5},{3,6},{4,7},{5,8},{6,9},{7,10},{8,11},{9,12},{10... | collective-permute-start | bytes 393224 | tf_op jit(solution)/shard_map/ppermute | solution.py:14
  14.1 3.9 %collective-permute-start = (bf16[256,256]{1,0:T(8,128)(2,1)}, bf16[256,256]{1,0:T(8,128)(2,1)}, u32[]{:S(2)}, u32[]{:S(2)}) collective-permute-start(bf16[256,256]{1,0:T(8,128)(2,1)} %constant_dynamic-update-slice_fusion), channel_id=1, source_target_pairs={{0,4},{1,5},{2,6},{3,7},{4,8},{5,9},{6,10},{7,11},{8,12},{9,13},{1... | collective-permute-start | bytes 393224 | tf_op jit(solution)/shard_map/ppermute | solution.py:14
  18.1 0.8 copy.23
  18.9 0.2 reduce-window.9
  19.0 0.1 reduce.4
  19.1 0.7 sub.49
  19.8 1.1 %fusion.48 = (bf16[128,1024]{1,0:T(8,128)(2,1)S(1)}, bf16[128,1024]{1,0:T(8,128)(2,1)S(1)}) fusion(bf16[256,1024]{1,0:T(8,128)(2,1)} %param.5), kind=kLoop, calls=%fused_computation.71 | loop fusion | bytes 1048576 | tf_op jit(solution)/shard_map/slice | solution.py:38
  20.9 0.2 select_reduce_fusion.1
  21.1 0.3 compare_and_fusion.1
  21.4 0.6 broadcast_bitcast_fusion.1
  22.0 0.6 broadcast_bitcast_fusion
  22.6 0.0 copy-start.3
  22.6 0.0 copy-start.4
  22.6 1.9 %fusion.47 = (bf16[128,1024]{1,0:T(8,128)(2,1)}, bf16[128,1024]{1,0:T(8,128)(2,1)}) fusion(bf16[256,1024]{1,0:T(8,128)(2,1)} %param.8), kind=kLoop, calls=%fused_computation.70 | loop fusion | bytes 1048576 | tf_op jit(solution)/shard_map/slice | solution.py:39
  24.5 0.1 reshape.203
  24.6 0.1 reshape.205
  24.8 1.1 %reshape.207 = bf16[1024,128]{1,0:T(8,128)(2,1)S(1)} reshape(bf16[128,1024]{1,0:T(8,128)(2,1)} %get-tuple-element.22) | data formatting | bytes 524288 | tf_op jit(solution)/shard_map/reshape | solution.py:39
  25.8 1.8 %reshape.209 = bf16[1024,128]{1,0:T(8,128)(2,1)} reshape(bf16[128,1024]{1,0:T(8,128)(2,1)} %get-tuple-element.23) | data formatting | bytes 524288 | tf_op jit(solution)/shard_map/reshape | solution.py:39
  27.6 1.8 %copy.31 = bf16[1024,128]{0,1:T(8,128)(2,1)} copy(bf16[1024,128]{1,0:T(8,128)(2,1)} %reshape.209) | data formatting | bytes 524288 | tf_op jit(solution)/shard_map/reshape | solution.py:39
  29.4 0.8 copy.30
  30.2 1.4 %copy.25 = pred[1024,1280]{0,1:T(32,128)(4,1)S(1)} copy(pred[1024,1280]{1,0:T(32,128)(4,1)S(1)} %broadcast_bitcast_fusion.1) | data formatting | bytes 2621440 | tf_op jit(solution)/shard_map/jit(_where)/broadcast_in_dim | solution.py:45
  31.7 1.4 %copy.28 = pred[1024,1280]{0,1:T(32,128)(4,1)S(1)} copy(pred[1024,1280]{1,0:T(32,128)(4,1)S(1)} %broadcast_bitcast_fusion) | data formatting | bytes 2621440 | tf_op jit(solution)/shard_map/jit(_where)/broadcast_in_dim | solution.py:45
  33.1 0.9 %constant_dynamic-update-slice_fusion.6 = bf16[1280,256]{1,0:T(8,128)(2,1)S(1)} fusion(bf16[256,256]{1,0:T(8,128)(2,1)} %collective-permute-done), kind=kLoop, calls=%fused_computation.64 | loop fusion | bytes 262144
  34.0 0.9 %constant_dynamic-update-slice_fusion.5 = bf16[1280,256]{1,0:T(8,128)(2,1)S(1)} fusion(bf16[1280,256]{1,0:T(8,128)(2,1)S(1)} %constant_dynamic-update-slice_fusion.6, bf16[256,256]{1,0:T(8,128)(2,1)} %collective-permute-done.1), kind=kLoop, calls=%fused_computation.63 | loop fusion | bytes 262144
  35.0 0.9 %constant_dynamic-update-slice_fusion.4 = bf16[1280,256]{1,0:T(8,128)(2,1)S(1)} fusion(bf16[1280,256]{1,0:T(8,128)(2,1)S(1)} %constant_dynamic-update-slice_fusion.5, bf16[256,256]{1,0:T(8,128)(2,1)} %collective-permute-done.2), kind=kLoop, calls=%fused_computation.62 | loop fusion | bytes 262144
  35.9 0.9 %constant_dynamic-update-slice_fusion.3 = bf16[1280,256]{1,0:T(8,128)(2,1)S(1)} fusion(bf16[1280,256]{1,0:T(8,128)(2,1)S(1)} %constant_dynamic-update-slice_fusion.4, bf16[256,256]{1,0:T(8,128)(2,1)} %collective-permute-done.3), kind=kLoop, calls=%fused_computation.61 | loop fusion | bytes 262144
  36.9 0.0 copy-start
  36.9 1.0 %fusion.4 = (f32[1024]{0:T(1024)S(1)}, f32[1280,1024]{1,0:T(8,128)S(1)}) fusion(pred[1024,1280]{0,1:T(32,128)(4,1)S(1)} %copy.28, bf16[1024,128]{1,0:T(8,128)(2,1)S(1)} %reshape.205, bf16[1280,256]{1,0:T(8,128)(2,1)S(1)} %constant_dynamic-update-slice_fusion.7), kind=kOutput, calls=%fused_computation.8 | convolution fusion | flops 339475456 | bytes 7147520 | tf_op jit(solution)/shard_map/dot_general | solution.py:40
  37.9 1.4 %fusion.13 = f32[1024]{0:T(1024)S(1)} fusion(pred[1024,1280]{0,1:T(32,128)(4,1)S(1)} %copy.28, f32[1280,1024]{1,0:T(8,128)S(1)} %get-tuple-element.31, f32[1024]{0:T(1024)S(1)} %get-tuple-element.30), kind=kLoop, calls=%fused_computation.19 | loop fusion | flops 5241856 | bytes 6561792 | tf_op jit(solution)/shard_map/reduce_sum | solution.py:46
  39.3 0.0 copy-start.2
  39.3 1.8 %fusion.14 = f32[1280,128]{0,1:T(8,128)S(1)} fusion(bf16[1024,128]{1,0:T(8,128)(2,1)S(1)} %copy-done, pred[1024,1280]{0,1:T(32,128)(4,1)S(1)} %copy.28, f32[1280,1024]{1,0:T(8,128)S(1)} %get-tuple-element.31, f32[1024]{0:T(1024)S(1)} %fusion.13, f32[1024]{0:T(1024)S(1)} %get-tuple-element.30), kind=kOutput, calls=%fused_computation.23 | convolution fusion | flops 342097920 | bytes 7479296 | tf_op jit(solution)/shard_map/dot_general | solution.py:65
  41.1 1.7 %multiply_reduce_fusion = (f32[1024]{0:T(1024)S(1)}, bf16[1024,128]{0,1:T(8,128)(2,1)S(1)}) fusion(bf16[1024,128]{0,1:T(8,128)(2,1)S(1)} %copy-done.2, bf16[1280,256]{1,0:T(8,128)(2,1)S(1)} %constant_dynamic-update-slice_fusion.7, f32[1024]{0:T(1024)S(1)} %fusion.13, pred[1024,1280]{0,1:T(32,128)(4,1)S(1)} %copy.28, f32[1024]{0:T(1024)S(1)} %get-tuple-element.30, ...), kind=kOutput, calls=%fused_computation.39 | convolution fusion | flops 342752256 | bytes 7417856 | tf_op jit(solution)/shard_map/dot_general | solution.py:49
  42.8 2.4 %fusion.1 = bf16[1024,1280]{0,1:T(8,128)(2,1)S(1)} fusion(bf16[1024,128]{1,0:T(8,128)(2,1)S(1)} %copy-done, f32[1024]{0:T(1024)S(1)} %get-tuple-element.34, bf16[1280,256]{1,0:T(8,128)(2,1)S(1)} %constant_dynamic-update-slice_fusion.7, f32[1024]{0:T(1024)S(1)} %fusion.13, pred[1024,1280]{0,1:T(32,128)(4,1)S(1)} %copy.28, f32[1024]{0:T(1024)S(1)} %get-tuple-element.30, ...), kind=kOutput, calls=%fused_computation.2 | convolution fusion | flops 346030080 | bytes 9777152 | tf_op jit(solution)/shard_map/dot_general | solution.py:52
  45.2 0.9 %convolution_convert_fusion = bf16[1024,128]{1,0:T(8,128)(2,1)S(1)} fusion(bf16[1024,1280]{0,1:T(8,128)(2,1)S(1)} %fusion.1, bf16[1280,256]{1,0:T(8,128)(2,1)S(1)} %constant_dynamic-update-slice_fusion.7), kind=kOutput, calls=%fused_computation.33 | convolution fusion | flops 335675392 | bytes 3211264 | tf_op jit(solution)/shard_map/dot_general | solution.py:59
  46.1 1.0 %fusion.51 = f32[1280,128]{0,1:T(8,128)S(1)} fusion(bf16[1024,1280]{0,1:T(8,128)(2,1)S(1)} %fusion.1, bf16[1024,128]{1,0:T(8,128)(2,1)S(1)} %reshape.205), kind=kOutput, calls=%fused_computation.74 | convolution fusion | flops 335544320 | bytes 3538944 | tf_op jit(solution)/shard_map/dot_general | solution.py:62
  47.1 1.0 %fusion.7 = (f32[1024]{0:T(1024)S(1)}, f32[1280,1024]{1,0:T(8,128)S(1)}) fusion(pred[1024,1280]{0,1:T(32,128)(4,1)S(1)} %copy.25, bf16[1024,128]{1,0:T(8,128)(2,1)S(1)} %reshape.203, bf16[1280,256]{1,0:T(8,128)(2,1)S(1)} %constant_dynamic-update-slice_fusion.7), kind=kOutput, calls=%fused_computation.13 | convolution fusion | flops 339475456 | bytes 7147520 | tf_op jit(solution)/shard_map/dot_general | solution.py:40
  48.2 1.4 %fusion.11 = f32[1024]{0:T(1024)S(1)} fusion(pred[1024,1280]{0,1:T(32,128)(4,1)S(1)} %copy.25, f32[1280,1024]{1,0:T(8,128)S(1)} %get-tuple-element.33, f32[1024]{0:T(1024)S(1)} %get-tuple-element.32), kind=kLoop, calls=%fused_computation.17 | loop fusion | flops 5241856 | bytes 6561792 | tf_op jit(solution)/shard_map/reduce_sum | solution.py:46
  49.6 1.8 %fusion.18 = f32[1280,128]{0,1:T(8,128)S(1)} fusion(bf16[1024,128]{1,0:T(8,128)(2,1)S(1)} %reshape.207, pred[1024,1280]{0,1:T(32,128)(4,1)S(1)} %copy.25, f32[1280,1024]{1,0:T(8,128)S(1)} %get-tuple-element.33, f32[1024]{0:T(1024)S(1)} %fusion.11, f32[1024]{0:T(1024)S(1)} %get-tuple-element.32), kind=kOutput, calls=%fused_computation.27 | convolution fusion | flops 342097920 | bytes 7479296 | tf_op jit(solution)/shard_map/dot_general | solution.py:65
  51.4 1.7 %multiply_reduce_fusion.1 = (f32[1024]{0:T(1024)S(1)}, bf16[1024,128]{0,1:T(8,128)(2,1)S(1)}) fusion(bf16[1024,128]{0,1:T(8,128)(2,1)S(1)} %copy-done.1, bf16[1280,256]{1,0:T(8,128)(2,1)S(1)} %constant_dynamic-update-slice_fusion.7, f32[1024]{0:T(1024)S(1)} %fusion.11, pred[1024,1280]{0,1:T(32,128)(4,1)S(1)} %copy.25, f32[1024]{0:T(1024)S(1)} %get-tuple-element.32, ...), kind=kOutput, calls=%fused_computation.40 | convolution fusion | flops 342752256 | bytes 7417856 | tf_op jit(solution)/shard_map/dot_general | solution.py:49
  53.1 2.2 %fusion.3 = bf16[1024,1280]{0,1:T(8,128)(2,1)S(1)} fusion(bf16[1024,128]{1,0:T(8,128)(2,1)S(1)} %reshape.207, f32[1024]{0:T(1024)S(1)} %get-tuple-element.36, bf16[1280,256]{1,0:T(8,128)(2,1)S(1)} %constant_dynamic-update-slice_fusion.7, f32[1024]{0:T(1024)S(1)} %fusion.11, pred[1024,1280]{0,1:T(32,128)(4,1)S(1)} %copy.25, f32[1024]{0:T(1024)S(1)} %get-tuple-element.32, ...), kind=kOutput, calls=%fused_computation.5 | convolution fusion | flops 346030080 | bytes 9777152 | tf_op jit(solution)/shard_map/dot_general | solution.py:52
  55.3 1.0 %fusion.50 = f32[1280,128]{0,1:T(8,128)S(1)} fusion(bf16[1024,1280]{0,1:T(8,128)(2,1)S(1)} %fusion.3, bf16[1024,128]{1,0:T(8,128)(2,1)S(1)} %reshape.203), kind=kOutput, calls=%fused_computation.73 | convolution fusion | flops 335544320 | bytes 3538944 | tf_op jit(solution)/shard_map/dot_general | solution.py:62
  56.3 0.1 maximum_add_fusion
  56.4 1.0 %fusion.46 = (f32[256,256]{0,1:T(8,128)}, f32[256,256]{0,1:T(8,128)}, f32[256,256]{0,1:T(8,128)}, f32[256,256]{0,1:T(8,128)}) fusion(f32[1280,256]{0,1:T(8,128)S(1)} %maximum_add_fusion), kind=kLoop, calls=%fused_computation.69 | loop fusion | bytes 2097152 | tf_op jit(solution)/shard_map/slice | solution.py:96
  57.5 5.0 %collective-permute-start.4 = (f32[256,256]{0,1:T(8,128)}, f32[256,256]{0,1:T(8,128)S(1)}, u32[]{:S(2)}, u32[]{:S(2)}) collective-permute-start(f32[256,256]{0,1:T(8,128)} %get-tuple-element.18), channel_id=1, source_target_pairs={{1,0},{2,1},{3,2},{4,3},{5,4},{6,5},{7,6},{8,7},{9,8},{10,9},{11,1... | collective-permute-start | bytes 786440 | tf_op jit(solution)/shard_map/ppermute | solution.py:14
  62.5 2.3 %collective-permute-start.7 = (f32[256,256]{0,1:T(8,128)}, f32[256,256]{0,1:T(8,128)S(1)}, u32[]{:S(2)}, u32[]{:S(2)}) collective-permute-start(f32[256,256]{0,1:T(8,128)} %get-tuple-element.19), channel_id=1, source_target_pairs={{4,0},{5,1},{6,2},{7,3},{8,4},{9,5},{10,6},{11,7},{12,8},{13,9},{1... | collective-permute-start | bytes 786440 | tf_op jit(solution)/shard_map/ppermute | solution.py:14
  64.7 3.8 %collective-permute-start.6 = (f32[256,256]{0,1:T(8,128)}, f32[256,256]{0,1:T(8,128)S(1)}, u32[]{:S(2)}, u32[]{:S(2)}) collective-permute-start(f32[256,256]{0,1:T(8,128)} %get-tuple-element.20), channel_id=1, source_target_pairs={{3,0},{4,1},{5,2},{6,3},{7,4},{8,5},{9,6},{10,7},{11,8},{12,9},{13... | collective-permute-start | bytes 786440 | tf_op jit(solution)/shard_map/ppermute | solution.py:14
  68.5 3.3 %collective-permute-start.5 = (f32[256,256]{0,1:T(8,128)}, f32[256,256]{0,1:T(8,128)}, u32[]{:S(2)}, u32[]{:S(2)}) collective-permute-start(f32[256,256]{0,1:T(8,128)} %get-tuple-element.21), channel_id=1, source_target_pairs={{2,0},{3,1},{4,2},{5,3},{6,4},{7,5},{8,6},{9,7},{10,8},{11,9},{12,... | collective-permute-start | bytes 786440 | tf_op jit(solution)/shard_map/ppermute | solution.py:14
  71.8 0.9 %convolution_convert_fusion.1 = bf16[1024,128]{1,0:T(8,128)(2,1)S(1)} fusion(bf16[1024,1280]{0,1:T(8,128)(2,1)S(1)} %fusion.3, bf16[1280,256]{1,0:T(8,128)(2,1)S(1)} %constant_dynamic-update-slice_fusion.7), kind=kOutput, calls=%fused_computation.34 | convolution fusion | flops 335675392 | bytes 3211264 | tf_op jit(solution)/shard_map/dot_general | solution.py:59
  72.7 0.2 copy.29
  72.9 0.1 reshape.206
  73.0 0.1 reshape.210
  73.1 0.2 copy.26
  73.3 0.1 reshape.204
  73.4 0.1 reshape.208
  73.6 0.8 pad_maximum_fusion
  74.4 0.8 pad_maximum_fusion.1
  75.2 6.8 %collective-permute-done.6 = f32[256,256]{0,1:T(8,128)S(1)} collective-permute-done((f32[256,256]{0,1:T(8,128)}, f32[256,256]{0,1:T(8,128)S(1)}, u32[]{:S(2)}, u32[]{:S(2)}) %collective-permute-start.6) | collective-permute-done | bytes 262176 | tf_op jit(solution)/shard_map/ppermute | solution.py:14
  82.1 1.0 %fusion.31 = bf16[256,256]{0,1:T(8,128)(2,1)S(1)} fusion(f32[256,256]{0,1:T(8,128)S(1)} %collective-permute-done.7, f32[256,256]{0,1:T(8,128)S(1)} %collective-permute-done.6, f32[256,256]{0,1:T(8,128)} %collective-permute-done.5, f32[256,256]{0,1:T(8,128)S(1)} %collective-permute-done.4, f32[1280,256]{0,1:T(8,128)S(1)} %maximum_add_fusion), kind=kLoop, calls=%fused_computation.45 | loop fusion | flops 327680 | bytes 1441792 | tf_op jit(solution)/shard_map/convert.1
  83.1 0.7 copy.33
  83.8 0.7 copy.32
  (18 shorter events, 0.1 us)
Async XLA Ops:
  3.6 32.3 %collective-permute-start.3 = (bf16[256,256]{1,0:T(8,128)(2,1)}, bf16[256,256]{1,0:T(8,128)(2,1)}, u32[]{:S(2)}, u32[]{:S(2)}) collective-permute-start(bf16[256,256]{1,0:T(8,128)(2,1)} %constant_dynamic-update-slice_fusion), channel_id=1, source_target_pairs={{0,1},{1,2},{2,3},{3,4},{4,5},{5,6},{6,7},{7,8},{8,9},{9,10},{10,1... | collective-permute-start | bytes 393224 | tf_op jit(solution)/shard_map/ppermute | solution.py:14
  7.0 28.0 %collective-permute-start.2 = (bf16[256,256]{1,0:T(8,128)(2,1)}, bf16[256,256]{1,0:T(8,128)(2,1)}, u32[]{:S(2)}, u32[]{:S(2)}) collective-permute-start(bf16[256,256]{1,0:T(8,128)(2,1)} %constant_dynamic-update-slice_fusion), channel_id=1, source_target_pairs={{0,2},{1,3},{2,4},{3,5},{4,6},{5,7},{6,8},{7,9},{8,10},{9,11},{10,... | collective-permute-start | bytes 393224 | tf_op jit(solution)/shard_map/ppermute | solution.py:14
  11.6 22.4 %collective-permute-start.1 = (bf16[256,256]{1,0:T(8,128)(2,1)}, bf16[256,256]{1,0:T(8,128)(2,1)}, u32[]{:S(2)}, u32[]{:S(2)}) collective-permute-start(bf16[256,256]{1,0:T(8,128)(2,1)} %constant_dynamic-update-slice_fusion), channel_id=1, source_target_pairs={{0,3},{1,4},{2,5},{3,6},{4,7},{5,8},{6,9},{7,10},{8,11},{9,12},{10... | collective-permute-start | bytes 393224 | tf_op jit(solution)/shard_map/ppermute | solution.py:14
  14.1 19.0 %collective-permute-start = (bf16[256,256]{1,0:T(8,128)(2,1)}, bf16[256,256]{1,0:T(8,128)(2,1)}, u32[]{:S(2)}, u32[]{:S(2)}) collective-permute-start(bf16[256,256]{1,0:T(8,128)(2,1)} %constant_dynamic-update-slice_fusion), channel_id=1, source_target_pairs={{0,4},{1,5},{2,6},{3,7},{4,8},{5,9},{6,10},{7,11},{8,12},{9,13},{1... | collective-permute-start | bytes 393224 | tf_op jit(solution)/shard_map/ppermute | solution.py:14
  22.6 14.2 %copy-start.3 = (bf16[256,128]{1,0:T(8,128)(2,1)S(1)}, bf16[256,128]{1,0:T(8,128)(2,1)}, u32[]{:S(2)}) copy-start(bf16[256,128]{1,0:T(8,128)(2,1)} %param.6) | copy-start | bytes 196612
  22.6 14.2 %copy-start.4 = (bf16[256,128]{1,0:T(8,128)(2,1)S(1)}, bf16[256,128]{1,0:T(8,128)(2,1)}, u32[]{:S(2)}) copy-start(bf16[256,128]{1,0:T(8,128)(2,1)} %param.7) | copy-start | bytes 196612
  36.9 2.4 %copy-start = (bf16[1024,128]{1,0:T(8,128)(2,1)S(1)}, bf16[1024,128]{1,0:T(8,128)(2,1)}, u32[]{:S(2)}) copy-start(bf16[1024,128]{1,0:T(8,128)(2,1)} %reshape.209) | copy-start | bytes 786436
  39.3 1.8 %copy-start.2 = (bf16[1024,128]{0,1:T(8,128)(2,1)S(1)}, bf16[1024,128]{0,1:T(8,128)(2,1)}, u32[]{:S(2)}) copy-start(bf16[1024,128]{0,1:T(8,128)(2,1)} %copy.31) | copy-start | bytes 786436
  49.5 1.8 %copy-start.1 = (bf16[1024,128]{0,1:T(8,128)(2,1)S(1)}, bf16[1024,128]{0,1:T(8,128)(2,1)}, u32[]{:S(2)}) copy-start(bf16[1024,128]{0,1:T(8,128)(2,1)} %copy.30) | copy-start | bytes 786436
  57.5 17.7 %collective-permute-start.4 = (f32[256,256]{0,1:T(8,128)}, f32[256,256]{0,1:T(8,128)S(1)}, u32[]{:S(2)}, u32[]{:S(2)}) collective-permute-start(f32[256,256]{0,1:T(8,128)} %get-tuple-element.18), channel_id=1, source_target_pairs={{1,0},{2,1},{3,2},{4,3},{5,4},{6,5},{7,6},{8,7},{9,8},{10,9},{11,1... | collective-permute-start | bytes 786440 | tf_op jit(solution)/shard_map/ppermute | solution.py:14
  62.5 12.7 %collective-permute-start.7 = (f32[256,256]{0,1:T(8,128)}, f32[256,256]{0,1:T(8,128)S(1)}, u32[]{:S(2)}, u32[]{:S(2)}) collective-permute-start(f32[256,256]{0,1:T(8,128)} %get-tuple-element.19), channel_id=1, source_target_pairs={{4,0},{5,1},{6,2},{7,3},{8,4},{9,5},{10,6},{11,7},{12,8},{13,9},{1... | collective-permute-start | bytes 786440 | tf_op jit(solution)/shard_map/ppermute | solution.py:14
  64.7 17.3 %collective-permute-start.6 = (f32[256,256]{0,1:T(8,128)}, f32[256,256]{0,1:T(8,128)S(1)}, u32[]{:S(2)}, u32[]{:S(2)}) collective-permute-start(f32[256,256]{0,1:T(8,128)} %get-tuple-element.20), channel_id=1, source_target_pairs={{3,0},{4,1},{5,2},{6,3},{7,4},{8,5},{9,6},{10,7},{11,8},{12,9},{13... | collective-permute-start | bytes 786440 | tf_op jit(solution)/shard_map/ppermute | solution.py:14
  68.5 13.6 %collective-permute-start.5 = (f32[256,256]{0,1:T(8,128)}, f32[256,256]{0,1:T(8,128)}, u32[]{:S(2)}, u32[]{:S(2)}) collective-permute-start(f32[256,256]{0,1:T(8,128)} %get-tuple-element.21), channel_id=1, source_target_pairs={{2,0},{3,1},{4,2},{5,3},{6,4},{7,5},{8,6},{9,7},{10,8},{11,9},{12,... | collective-permute-start | bytes 786440 | tf_op jit(solution)/shard_map/ppermute | solution.py:14
where the time goes:
time: 85.2 us; the launch traced here: 84.6 us
  starting transfers between devices  28.8 us (34%)
  local copies, waits for them, and re-layouts  23.4 us (27%)
  matrix products  17.4 us (20%)
  other arithmetic  7.01 us (8%)
  waiting for transfers between devices  6.85 us (8%)
  between operations  1.08 us (1%)
    ppermute x8, starting transfers between devices, passed_along(): return lax.ppermute(block, axis, route)  28.8 us
    ppermute x8, waiting for transfers between devices, passed_along(): return lax.ppermute(block, axis, route)  6.85 us
    unnamed x18, local copies, waits for them, and re-layouts  6.64 us
    reshape x4, local copies, waits for them, and re-layouts, window_attention(): grad_part[low:low + step_rows].reshape(step_rows * heads, head_dim)  5.46 us
    dot_general x2, matrix products, window_attention(): lax.dot_general(grad_flat, values_win, (((1,), (1,)), ((), ())), preferre...  4.59 us
    broadcast_in_dim x4, local copies, waits for them, and re-layouts, window_attention(): weights = jnp.exp(jnp.where(mask_three, scores - highest, -jnp.inf))  4.04 us
    dot_general x2, matrix products, window_attention(): lax.dot_general(probs_low, grad_flat, (((0,), (0,)), ((), ())), preferred...  3.57 us
    dot_general x2, matrix products, window_attention(): jnp.dot(probs_low, values_win, preferred_element_type=jnp.float32)  3.42 us
  transfers between devices with their start and end apart: 8, of which 1 were waited for; matrix products, arithmetic and copies ran while one was open for 25% of the time, Pallas kernels for 0%

commit v1 on v0

v1 whole, which is shorter than its diff:
```python
import functools, math
import jax
import jax.numpy as jnp
from jax import lax
from jax.experimental import pallas as pl
from jax.experimental.pallas import tpu as pltpu
from jax.sharding import PartitionSpec as P

F32, BF16 = jnp.float32, jnp.bfloat16
NT = (((1,), (1,)), ((), ()))
NN = (((1,), (0,)), ((), ()))
LOG2E = 1.4426950408889634

def attention_kernel(lens_ref, q_ref, do_ref, k_ref, v_ref, *refs, first_of, unroll):
    reach = 4
    far = refs[:reach]
    out_ref, dq_ref = refs[reach:reach + 2]
    back = refs[reach + 2:2 * reach + 2]
    mine_ref, bias, s_buf, dp_buf, p_buf, ds_buf, qs, dos, vt, kt = refs[2 * reach + 2:]
    rows, hd = k_ref.shape
    heads = q_ref.shape[1] // hd
    nb = reach + 1
    width = nb * rows
    factor = 1.0 / math.sqrt(hd)
    q0 = first_of()
    nd = lens_ref.shape[1]
    lens = lens_ref[...]
    di = lax.broadcasted_iota(jnp.int32, (nd, nd), 0)
    dj = lax.broadcasted_iota(jnp.int32, (nd, nd), 1)
    ends = jnp.sum(jnp.where(dj <= di, lens, 0), axis=1, keepdims=True)
    mylen = jnp.sum(jnp.where(dj == di, lens, 0), axis=1, keepdims=True)
    qpos = q0 + lax.broadcasted_iota(jnp.int32, (1, rows), 1)
    begin = jnp.sum(jnp.where(ends <= qpos, mylen, 0), axis=0, keepdims=True)
    def kv(b):
        if b == reach:
            return k_ref[...], v_ref[...]
        return far[b][0:rows, :], far[b][rows:, :]
    for b in range(nb):
        kpos = q0 + (b - reach) * rows + lax.broadcasted_iota(jnp.int32, (rows, 1), 0)
        bias[b * rows:(b + 1) * rows, :] = jnp.where((kpos >= begin) & (kpos <= qpos), 0.0, -jnp.inf)
        k, v = kv(b)
        kt[:, b * rows:(b + 1) * rows] = k.T
        vt[:, b * rows:(b + 1) * rows] = v.T
    def head(h):
        hs = pl.ds(pl.multiple_of(h * hd, hd), hd) if not isinstance(h, int) else slice(h * hd, (h + 1) * hd)
        ps = pl.ds(pl.multiple_of(h * rows, rows), rows) if not isinstance(h, int) else slice(h * rows, (h + 1) * rows)
        q = q_ref[:, hs]
        do = do_ref[:, hs]
        qs[ps, :] = q
        dos[ps, :] = do
        m = jnp.full((8, rows), -jnp.inf, F32)
        for b in range(nb):
            bs = slice(b * rows, (b + 1) * rows)
            k, v = kv(b)
            s = lax.dot_general(k, q, NT, preferred_element_type=F32) * (factor * LOG2E) + bias[bs, :]
            s_buf[bs, :] = s
            m = jnp.maximum(m, jnp.max(s.reshape(rows // 8, 8, rows), axis=0))
            dp_buf[bs, :] = lax.dot_general(v, do, NT, preferred_element_type=F32)
        m = jnp.max(m, axis=0, keepdims=True)
        l = jnp.zeros((8, rows), F32)
        t = jnp.zeros((8, rows), F32)
        for b in range(nb):
            bs = slice(b * rows, (b + 1) * rows)
            p = jnp.exp2(s_buf[bs, :] - m)
            s_buf[bs, :] = p
            l = l + jnp.sum(p.reshape(rows // 8, 8, rows), axis=0)
            t = t + jnp.sum((p * dp_buf[bs, :]).reshape(rows // 8, 8, rows), axis=0)
        inv = 1.0 / jnp.sum(l, axis=0, keepdims=True)
        delta = jnp.sum(t, axis=0, keepdims=True) * inv
        for b in range(nb):
            bs = slice(b * rows, (b + 1) * rows)
            p = s_buf[bs, :] * inv
            p_buf[bs, ps] = p.astype(BF16)
            ds_buf[bs, ps] = (p * (dp_buf[bs, :] - delta)).astype(BF16)
        o = lax.dot_general(vt[...], p_buf[:, ps], NN, preferred_element_type=F32)
        out_ref[:, hs] = o.T.astype(BF16)
        dq = lax.dot_general(kt[...], ds_buf[:, ps], NN, preferred_element_type=F32) * factor
        dq_ref[:, hs] = dq.T.astype(BF16)
    if unroll:
        for h in range(heads):
            head(h)
    else:
        @pl.loop(0, heads)
        def _(h):
            head(h)
    for b in range(nb):
        bs = slice(b * rows, (b + 1) * rows)
        dv = lax.dot_general(p_buf[bs, :], dos[...], NN, preferred_element_type=F32)
        dk = lax.dot_general(ds_buf[bs, :], qs[...], NN, preferred_element_type=F32) * factor
        ref = mine_ref if b == reach else back[b]
        ref[0:rows, :] = dk.astype(ref.dtype)
        ref[rows:, :] = dv.astype(ref.dtype)

def attention(lens, q, do, k, v, far, first_of, unroll=False):
    rows, hd = k.shape
    reach = len(far)
    width = (reach + 1) * rows
    heads = q.shape[1] // hd
    sd = jax.ShapeDtypeStruct
    vm = pl.BlockSpec(memory_space=pltpu.VMEM)
    return pl.pallas_call(
        functools.partial(attention_kernel, first_of=first_of, unroll=unroll),
        out_shape=[sd(q.shape, BF16), sd(q.shape, BF16)] + [sd((2 * rows, hd), BF16)] * reach + [sd((2 * rows, hd), F32)],
        in_specs=[vm] * (5 + reach),
        out_specs=[vm] * (3 + reach),
        scratch_shapes=[
            pltpu.VMEM((width, rows), F32), pltpu.VMEM((width, rows), F32), pltpu.VMEM((width, rows), F32),
            pltpu.VMEM((width, heads * rows), BF16), pltpu.VMEM((width, heads * rows), BF16),
            pltpu.VMEM((heads * rows, hd), BF16), pltpu.VMEM((heads * rows, hd), BF16),
            pltpu.VMEM((hd, width), BF16), pltpu.VMEM((hd, width), BF16),
        ],
        compiler_params=pltpu.CompilerParams(vmem_limit_bytes=48 * 2**20),
        name="window",
    )(lens.reshape(1, -1), q, do, k, v, *far)


REACH = 4


def shifted(block, distance):
    count = lax.axis_size("ctx") * lax.axis_size("grp")
    route = [(i, (i + distance) % count) for i in range(count)]
    return lax.ppermute(block, ("ctx", "grp"), route)


def body(queries, key_rows, value_rows, out_grad, doc_lengths):
    rows, hd = key_rows.shape

    def first_of():
        return (lax.axis_index("ctx") * lax.axis_size("grp") + lax.axis_index("grp")) * rows

    packed = jnp.concatenate([key_rows, value_rows], axis=0)
    far = [shifted(packed, d) for d in range(REACH, 0, -1)]
    attended, query_grad, *parts = attention(
        doc_lengths, queries, out_grad, key_rows, value_rows, far, first_of, True
    )
    total = parts[-1]
    for d in range(REACH, 0, -1):
        total = total + shifted(parts[REACH - d], -d).astype(F32)
    total = total.astype(BF16)
    return attended, query_grad, total[:rows], total[rows:]


def solution(mesh):
    split = P(("ctx", "grp"), None)
    return jax.shard_map(
        body, mesh=mesh, in_specs=(split,) * 4 + (P(),), out_specs=(split,) * 4, check_vma=False
    )
```

time: 85.2 us -> 47.2 us (0.55)
  the two profiles are of different devices: /device:TPU:16 before, /device:TPU:1 now
where the time goes in v1:
time: 47.2 us; the launch traced here: 46.6 us
  starting transfers between devices  21.9 us (46%)
  Pallas kernels  13.2 us (28%)
  waiting for transfers between devices  6.99 us (15%)
  local copies, waits for them, and re-layouts  3.65 us (8%)
  between operations  0.68 us (1%)
    ppermute x8, starting transfers between devices, shifted(): return lax.ppermute(block, ('ctx', 'grp'), route)  21.9 us
    pallas_call x1, Pallas kernels, attention(): pl.pallas_call(functools.partial(attention_kernel, first_of=first_of, unr...  13.2 us
    ppermute x8, waiting for transfers between devices, shifted(): return lax.ppermute(block, ('ctx', 'grp'), route)  6.99 us
    unnamed x11, local copies, waits for them, and re-layouts  2.97 us
  transfers between devices with their start and end apart: 8, of which 4 were waited for; matrix products, arithmetic and copies ran while one was open for 0% of the time, Pallas kernels for 0%

profile of v1, /device:TPU:1, one launch (start us, length us, event | category | flops | bytes accessed | tf_op | source)
XLA Modules:
  0.0 46.6 jit_solution(7487462597516939633)
XLA Ops:
  0.6 0.0 copy-start.3
  0.6 0.9 %constant_dynamic-update-slice_fusion.1 = bf16[512,128]{1,0:T(8,128)(2,1)S(1)} fusion(bf16[256,128]{1,0:T(8,128)(2,1)} %k_ref.1), kind=kLoop, calls=%fused_computation.2 | loop fusion | bytes 131072
  1.5 0.0 copy-done.3
  1.5 0.0 copy-start.2
  1.5 0.0 copy-start.4
  1.6 2.1 %collective-permute-start.3 = (bf16[512,128]{1,0:T(8,128)(2,1)S(1)}, bf16[512,128]{1,0:T(8,128)(2,1)S(1)}, u32[]{:S(2)}, u32[]{:S(2)}) collective-permute-start(bf16[512,128]{1,0:T(8,128)(2,1)S(1)} %constant_dynamic-update-slice_fusion), channel_id=1, source_target_pairs={{0,1},{1,2},{2,3},{3,4},{4,5},{5,6},{6,7},{7,8},{8,9},{9,10},{10,1... | collective-permute-start | bytes 393224 | tf_op jit(solution)/shard_map/ppermute | solution.py:123
  3.7 2.5 %collective-permute-start.2 = (bf16[512,128]{1,0:T(8,128)(2,1)S(1)}, bf16[512,128]{1,0:T(8,128)(2,1)S(1)}, u32[]{:S(2)}, u32[]{:S(2)}) collective-permute-start(bf16[512,128]{1,0:T(8,128)(2,1)S(1)} %constant_dynamic-update-slice_fusion), channel_id=1, source_target_pairs={{0,2},{1,3},{2,4},{3,5},{4,6},{5,7},{6,8},{7,9},{8,10},{9,11},{10,... | collective-permute-start | bytes 393224 | tf_op jit(solution)/shard_map/ppermute | solution.py:123
  6.1 3.3 %collective-permute-start.1 = (bf16[512,128]{1,0:T(8,128)(2,1)S(1)}, bf16[512,128]{1,0:T(8,128)(2,1)S(1)}, u32[]{:S(2)}, u32[]{:S(2)}) collective-permute-start(bf16[512,128]{1,0:T(8,128)(2,1)S(1)} %constant_dynamic-update-slice_fusion), channel_id=1, source_target_pairs={{0,3},{1,4},{2,5},{3,6},{4,7},{5,8},{6,9},{7,10},{8,11},{9,12},{10... | collective-permute-start | bytes 393224 | tf_op jit(solution)/shard_map/ppermute | solution.py:123
  9.5 0.0 collective-permute-start
  9.5 0.0 collective-permute-done.3.refs_3_
  9.5 1.9 %collective-permute-done.2.refs_2_ = bf16[512,128]{1,0:T(8,128)(2,1)S(1)} collective-permute-done((bf16[512,128]{1,0:T(8,128)(2,1)S(1)}, bf16[512,128]{1,0:T(8,128)(2,1)S(1)}, u32[]{:S(2)}, u32[]{:S(2)}) %collective-permute-start.2) | collective-permute-done | bytes 131104 | tf_op jit(solution)/shard_map/ppermute | solution.py:123
  11.4 1.2 %collective-permute-done.1.refs_1_ = bf16[512,128]{1,0:T(8,128)(2,1)S(1)} collective-permute-done((bf16[512,128]{1,0:T(8,128)(2,1)S(1)}, bf16[512,128]{1,0:T(8,128)(2,1)S(1)}, u32[]{:S(2)}, u32[]{:S(2)}) %collective-permute-start.1) | collective-permute-done | bytes 131104 | tf_op jit(solution)/shard_map/ppermute | solution.py:123
  12.6 0.0 collective-permute-done.refs_0_
  12.6 0.0 copy-done.2
  12.6 0.0 copy-done.4
  12.6 0.0 copy-start
  12.6 1.0 %copy-done = bf16[256,1024]{1,0:T(8,128)(2,1)S(1)} copy-done((bf16[256,1024]{1,0:T(8,128)(2,1)S(1)}, bf16[256,1024]{1,0:T(8,128)(2,1)}, u32[]{:S(2)}) %copy-start) | copy-done | bytes 524312
  13.7 0.0 copy-start.1
  13.7 1.0 %copy-done.1 = bf16[256,1024]{1,0:T(8,128)(2,1)S(1)} copy-done((bf16[256,1024]{1,0:T(8,128)(2,1)S(1)}, bf16[256,1024]{1,0:T(8,128)(2,1)}, u32[]{:S(2)}) %copy-start.1) | copy-done | bytes 524312
  14.7 13.2 %window.1 = (bf16[256,1024]{1,0:T(8,128)(2,1)}, bf16[256,1024]{1,0:T(8,128)(2,1)}, bf16[512,128]{1,0:T(8,128)(2,1)S(1)}, bf16[512,128]{1,0:T(8,128)(2,1)S(1)}, b...) custom-call(s32[1,128]{1,0:T(1,128)S(1)} %bitcast.1, ...), custom_call_target="tpu_custom_call" | custom-call | tf_op jit(solution)/shard_map/window/pallas_call | solution.py:101
  27.9 7.4 %collective-permute-start.4 = (bf16[512,128]{1,0:T(8,128)(2,1)S(1)}, bf16[512,128]{1,0:T(8,128)(2,1)S(1)}, u32[]{:S(2)}, u32[]{:S(2)}) collective-permute-start(bf16[512,128]{1,0:T(8,128)(2,1)S(1)} %get-tuple-element.14), channel_id=1, source_target_pairs={{0,252},{1,253},{2,254},{3,255},{4,0},{5,1},{6,2},{7,3},{8,4},{9,5... | collective-permute-start | bytes 393224 | tf_op jit(solution)/shard_map/ppermute | solution.py:123
  35.4 2.5 %collective-permute-start.5 = (bf16[512,128]{1,0:T(8,128)(2,1)S(1)}, bf16[512,128]{1,0:T(8,128)(2,1)S(1)}, u32[]{:S(2)}, u32[]{:S(2)}) collective-permute-start(bf16[512,128]{1,0:T(8,128)(2,1)S(1)} %get-tuple-element.15), channel_id=1, source_target_pairs={{0,253},{1,254},{2,255},{3,0},{4,1},{5,2},{6,3},{7,4},{8,5},{9,6},... | collective-permute-start | bytes 393224 | tf_op jit(solution)/shard_map/ppermute | solution.py:123
  37.9 2.4 %collective-permute-start.6 = (bf16[512,128]{1,0:T(8,128)(2,1)S(1)}, bf16[512,128]{1,0:T(8,128)(2,1)S(1)}, u32[]{:S(2)}, u32[]{:S(2)}) collective-permute-start(bf16[512,128]{1,0:T(8,128)(2,1)S(1)} %get-tuple-element.16), channel_id=1, source_target_pairs={{0,254},{1,255},{2,0},{3,1},{4,2},{5,3},{6,4},{7,5},{8,6},{9,7},{1... | collective-permute-start | bytes 393224 | tf_op jit(solution)/shard_map/ppermute | solution.py:123
  40.3 1.6 %collective-permute-start.7 = (bf16[512,128]{1,0:T(8,128)(2,1)S(1)}, bf16[512,128]{1,0:T(8,128)(2,1)S(1)}, u32[]{:S(2)}, u32[]{:S(2)}) collective-permute-start(bf16[512,128]{1,0:T(8,128)(2,1)S(1)} %get-tuple-element.17), channel_id=1, source_target_pairs={{0,255},{1,0},{2,1},{3,2},{4,3},{5,4},{6,5},{7,6},{8,7},{9,8},{10,... | collective-permute-start | bytes 393224 | tf_op jit(solution)/shard_map/ppermute | solution.py:123
  41.9 0.0 collective-permute-done.4
  42.0 0.0 collective-permute-done.5
  42.0 2.8 %collective-permute-done.6 = bf16[512,128]{1,0:T(8,128)(2,1)S(1)} collective-permute-done((bf16[512,128]{1,0:T(8,128)(2,1)S(1)}, bf16[512,128]{1,0:T(8,128)(2,1)S(1)}, u32[]{:S(2)}, u32[]{:S(2)}) %collective-permute-start.6) | collective-permute-done | bytes 131104 | tf_op jit(solution)/shard_map/ppermute | solution.py:123
  44.8 1.1 %collective-permute-done.7 = bf16[512,128]{1,0:T(8,128)(2,1)S(1)} collective-permute-done((bf16[512,128]{1,0:T(8,128)(2,1)S(1)}, bf16[512,128]{1,0:T(8,128)(2,1)S(1)}, u32[]{:S(2)}, u32[]{:S(2)}) %collective-permute-start.7) | collective-permute-done | bytes 131104 | tf_op jit(solution)/shard_map/ppermute | solution.py:123
  45.8 0.1 add_convert_fusion
  45.9 0.7 %fusion = (bf16[256,128]{1,0:T(8,128)(2,1)}, bf16[256,128]{1,0:T(8,128)(2,1)}) fusion(bf16[512,128]{1,0:T(8,128)(2,1)S(1)} %add_convert_fusion), kind=kLoop, calls=%fused_computation.3 | loop fusion | bytes 262144 | tf_op jit(solution)/shard_map/slice | solution.py:141
  (1 shorter events, 0.0 us)
Async XLA Ops:
  0.6 0.9 %copy-start.3 = (bf16[256,128]{1,0:T(8,128)(2,1)S(1)}, bf16[256,128]{1,0:T(8,128)(2,1)}, u32[]{:S(2)}) copy-start(bf16[256,128]{1,0:T(8,128)(2,1)} %v_ref.1) | copy-start | bytes 196612
  1.5 11.1 %copy-start.2 = (bf16[256,128]{1,0:T(8,128)(2,1)S(1)}, bf16[256,128]{1,0:T(8,128)(2,1)}, u32[]{:S(2)}) copy-start(bf16[256,128]{1,0:T(8,128)(2,1)} %k_ref.1) | copy-start | bytes 196612
  1.5 11.1 %copy-start.4 = (s32[128]{0:T(128)S(1)}, s32[128]{0:T(128)}, u32[]{:S(2)}) copy-start(s32[128]{0:T(128)} %param.9) | copy-start | bytes 1540
  1.6 7.9 %collective-permute-start.3 = (bf16[512,128]{1,0:T(8,128)(2,1)S(1)}, bf16[512,128]{1,0:T(8,128)(2,1)S(1)}, u32[]{:S(2)}, u32[]{:S(2)}) collective-permute-start(bf16[512,128]{1,0:T(8,128)(2,1)S(1)} %constant_dynamic-update-slice_fusion), channel_id=1, source_target_pairs={{0,1},{1,2},{2,3},{3,4},{4,5},{5,6},{6,7},{7,8},{8,9},{9,10},{10,1... | collective-permute-start | bytes 393224 | tf_op jit(solution)/shard_map/ppermute | solution.py:123
  3.7 7.7 %collective-permute-start.2 = (bf16[512,128]{1,0:T(8,128)(2,1)S(1)}, bf16[512,128]{1,0:T(8,128)(2,1)S(1)}, u32[]{:S(2)}, u32[]{:S(2)}) collective-permute-start(bf16[512,128]{1,0:T(8,128)(2,1)S(1)} %constant_dynamic-update-slice_fusion), channel_id=1, source_target_pairs={{0,2},{1,3},{2,4},{3,5},{4,6},{5,7},{6,8},{7,9},{8,10},{9,11},{10,... | collective-permute-start | bytes 393224 | tf_op jit(solution)/shard_map/ppermute | solution.py:123
  6.1 6.5 %collective-permute-start.1 = (bf16[512,128]{1,0:T(8,128)(2,1)S(1)}, bf16[512,128]{1,0:T(8,128)(2,1)S(1)}, u32[]{:S(2)}, u32[]{:S(2)}) collective-permute-start(bf16[512,128]{1,0:T(8,128)(2,1)S(1)} %constant_dynamic-update-slice_fusion), channel_id=1, source_target_pairs={{0,3},{1,4},{2,5},{3,6},{4,7},{5,8},{6,9},{7,10},{8,11},{9,12},{10... | collective-permute-start | bytes 393224 | tf_op jit(solution)/shard_map/ppermute | solution.py:123
  9.5 3.1 %collective-permute-start = (bf16[512,128]{1,0:T(8,128)(2,1)S(1)}, bf16[512,128]{1,0:T(8,128)(2,1)S(1)}, u32[]{:S(2)}, u32[]{:S(2)}) collective-permute-start(bf16[512,128]{1,0:T(8,128)(2,1)S(1)} %constant_dynamic-update-slice_fusion), channel_id=1, source_target_pairs={{0,4},{1,5},{2,6},{3,7},{4,8},{5,9},{6,10},{7,11},{8,12},{9,13},{1... | collective-permute-start | bytes 393224 | tf_op jit(solution)/shard_map/ppermute | solution.py:123
  12.6 1.0 %copy-start = (bf16[256,1024]{1,0:T(8,128)(2,1)S(1)}, bf16[256,1024]{1,0:T(8,128)(2,1)}, u32[]{:S(2)}) copy-start(bf16[256,1024]{1,0:T(8,128)(2,1)} %q_ref.1) | copy-start | bytes 1572868
  13.7 1.0 %copy-start.1 = (bf16[256,1024]{1,0:T(8,128)(2,1)S(1)}, bf16[256,1024]{1,0:T(8,128)(2,1)}, u32[]{:S(2)}) copy-start(bf16[256,1024]{1,0:T(8,128)(2,1)} %do_ref.1) | copy-start | bytes 1572868
  27.9 14.0 %collective-permute-start.4 = (bf16[512,128]{1,0:T(8,128)(2,1)S(1)}, bf16[512,128]{1,0:T(8,128)(2,1)S(1)}, u32[]{:S(2)}, u32[]{:S(2)}) collective-permute-start(bf16[512,128]{1,0:T(8,128)(2,1)S(1)} %get-tuple-element.14), channel_id=1, source_target_pairs={{0,252},{1,253},{2,254},{3,255},{4,0},{5,1},{6,2},{7,3},{8,4},{9,5... | collective-permute-start | bytes 393224 | tf_op jit(solution)/shard_map/ppermute | solution.py:123
  35.4 6.6 %collective-permute-start.5 = (bf16[512,128]{1,0:T(8,128)(2,1)S(1)}, bf16[512,128]{1,0:T(8,128)(2,1)S(1)}, u32[]{:S(2)}, u32[]{:S(2)}) collective-permute-start(bf16[512,128]{1,0:T(8,128)(2,1)S(1)} %get-tuple-element.15), channel_id=1, source_target_pairs={{0,253},{1,254},{2,255},{3,0},{4,1},{5,2},{6,3},{7,4},{8,5},{9,6},... | collective-permute-start | bytes 393224 | tf_op jit(solution)/shard_map/ppermute | solution.py:123
  37.9 6.9 %collective-permute-start.6 = (bf16[512,128]{1,0:T(8,128)(2,1)S(1)}, bf16[512,128]{1,0:T(8,128)(2,1)S(1)}, u32[]{:S(2)}, u32[]{:S(2)}) collective-permute-start(bf16[512,128]{1,0:T(8,128)(2,1)S(1)} %get-tuple-element.16), channel_id=1, source_target_pairs={{0,254},{1,255},{2,0},{3,1},{4,2},{5,3},{6,4},{7,5},{8,6},{9,7},{1... | collective-permute-start | bytes 393224 | tf_op jit(solution)/shard_map/ppermute | solution.py:123
  40.3 5.5 %collective-permute-start.7 = (bf16[512,128]{1,0:T(8,128)(2,1)S(1)}, bf16[512,128]{1,0:T(8,128)(2,1)S(1)}, u32[]{:S(2)}, u32[]{:S(2)}) collective-permute-start(bf16[512,128]{1,0:T(8,128)(2,1)S(1)} %get-tuple-element.17), channel_id=1, source_target_pairs={{0,255},{1,0},{2,1},{3,2},{4,3},{5,4},{6,5},{7,6},{8,7},{9,8},{10,... | collective-permute-start | bytes 393224 | tf_op jit(solution)/shard_map/ppermute | solution.py:123

commit v2 on v1

v2 whole, which is shorter than its diff:
```python
import functools
import math

import jax
import jax.numpy as jnp
from jax import lax
from jax.experimental import pallas as pl
from jax.experimental.pallas import tpu as pltpu
from jax.sharding import PartitionSpec as P

F32, BF16 = jnp.float32, jnp.bfloat16
NT = (((1,), (1,)), ((), ()))
NN = (((1,), (0,)), ((), ()))
LOG2E = 1.4426950408889634
REACH = 4
CHUNK = 64


def dot(a, b, dims):
    return lax.dot_general(a, b, dims, preferred_element_type=F32)


def fold(x, op):
    return op(x.reshape(x.shape[0] // 8, 8, x.shape[1]), axis=0)


def local_kernel(lens_ref, q_ref, do_ref, k_ref, v_ref, qs, dos, bias, st_ref, *, first_of):
    heads, rows, hd = qs.shape
    scale = LOG2E / math.sqrt(hd)
    q0 = first_of()
    nd = lens_ref.shape[1]
    lens = lens_ref[...]
    di = lax.broadcasted_iota(jnp.int32, (nd, nd), 0)
    dj = lax.broadcasted_iota(jnp.int32, (nd, nd), 1)
    ends = jnp.sum(jnp.where(dj <= di, lens, 0), axis=1, keepdims=True)
    length = jnp.sum(jnp.where(dj == di, lens, 0), axis=1, keepdims=True)
    qpos = q0 + lax.broadcasted_iota(jnp.int32, (1, rows), 1)
    begin = jnp.sum(jnp.where(ends <= qpos, length, 0), axis=0, keepdims=True)
    for b in range(REACH + 1):
        kpos = q0 + (b - REACH) * rows + lax.broadcasted_iota(jnp.int32, (rows, 1), 0)
        bias[b * rows : (b + 1) * rows, :] = jnp.where(
            (kpos >= begin) & (kpos <= qpos), 0.0, -jnp.inf
        )
    for h in range(heads):
        q = q_ref[:, h * hd : (h + 1) * hd]
        do = do_ref[:, h * hd : (h + 1) * hd]
        qs[h] = q
        dos[h] = do
        s = dot(k_ref[...], q, NT) * scale + bias[REACH * rows :, :]
        m = jnp.max(fold(s, jnp.max), axis=0, keepdims=True)
        p = jnp.exp2(s - m)
        dp = dot(v_ref[...], do, NT)
        st_ref[h, 0:1, :] = m
        st_ref[h, 1:2, :] = jnp.sum(fold(p, jnp.sum), axis=0, keepdims=True)
        st_ref[h, 2:3, :] = jnp.sum(fold(p * dp, jnp.sum), axis=0, keepdims=True)


def remote_kernel(q_ref, do_ref, bias, st_ref, *refs):
    far = refs[:REACH]
    back = refs[REACH : 2 * REACH]
    p_out, ds_out, st_out, kall, vall, s_buf, dp_buf, m_buf, dv_acc, dk_acc = refs[2 * REACH :]
    heads, rows, hd = q_ref.shape
    width = REACH * rows
    factor = 1.0 / math.sqrt(hd)
    scale = factor * LOG2E
    for b in range(REACH):
        kall[b * rows : (b + 1) * rows, :] = far[b][0:rows, :]
        vall[b * rows : (b + 1) * rows, :] = far[b][rows:, :]
    chunks = [slice(c, c + CHUNK) for c in range(0, width, CHUNK)]

    def scores(h):
        s = dot(kall[...], q_ref[h], NT)
        dp = dot(vall[...], do_ref[h], NT)
        m = jnp.full((8, rows), -jnp.inf, F32)
        for cs in chunks:
            x = s[cs, :] * scale + bias[cs, :]
            m = jnp.maximum(m, fold(x, jnp.max))
            s_buf[cs, :] = x
            dp_buf[cs, :] = dp[cs, :]
        m_buf[...] = m

    def statistics(h):
        m0 = st_ref[h, 0:1, :]
        m = jnp.maximum(m0, jnp.max(m_buf[...], axis=0, keepdims=True))
        w0 = jnp.exp2(m0 - m)
        l = jnp.zeros((8, rows), F32)
        t = jnp.zeros((8, rows), F32)
        for cs in chunks:
            p = jnp.exp2(s_buf[cs, :] - m)
            l = l + fold(p, jnp.sum)
            t = t + fold(p * dp_buf[cs, :], jnp.sum)
        total = jnp.sum(l, axis=0, keepdims=True) + w0 * st_ref[h, 1:2, :]
        delta = (jnp.sum(t, axis=0, keepdims=True) + w0 * st_ref[h, 2:3, :]) / total
        lse = m + jnp.log2(total)
        st_out[h, 0:1, :] = lse
        st_out[h, 1:2, :] = delta
        return lse, delta

    def weights(h, lse, delta):
        for cs in chunks:
            p = jnp.exp2(s_buf[cs, :] - lse)
            p_out[h, cs, :] = p.astype(BF16)
            ds_out[h, cs, :] = (p * (dp_buf[cs, :] - delta)).astype(BF16)

    def grads(h):
        dv_acc[...] += dot(p_out[h], do_ref[h], NN)
        dk_acc[...] += dot(ds_out[h], q_ref[h], NN)

    dv_acc[...] = jnp.zeros_like(dv_acc)
    dk_acc[...] = jnp.zeros_like(dk_acc)
    scores(0)
    weights(0, *statistics(0))
    scores(1)

    @pl.loop(1, heads - 1)
    def _(h):
        grads(h - 1)
        weights(h, *statistics(h))
        scores(h + 1)

    grads(heads - 2)
    weights(heads - 1, *statistics(heads - 1))
    grads(heads - 1)
    for b in range(REACH):
        bs = slice(b * rows, (b + 1) * rows)
        back[b][0:rows, :] = (dk_acc[bs, :] * factor).astype(BF16)
        back[b][rows:, :] = dv_acc[bs, :].astype(BF16)


def own_kernel(q_ref, do_ref, bias, st_ref, p_ref, ds_ref, k_ref, v_ref, *refs):
    far = refs[:REACH]
    out_ref, dq_ref, mine_ref, kt, vt = refs[REACH:]
    heads, rows, hd = q_ref.shape
    width = REACH * rows
    factor = 1.0 / math.sqrt(hd)
    scale = factor * LOG2E
    for b in range(REACH):
        kt[:, b * rows : (b + 1) * rows] = far[b][0:rows, :].T
        vt[:, b * rows : (b + 1) * rows] = far[b][rows:, :].T
    kt[:, width:] = k_ref[...].T
    vt[:, width:] = v_ref[...].T
    dk = dv = None
    for h in range(heads):
        hs = slice(h * hd, (h + 1) * hd)
        q = q_ref[h]
        do = do_ref[h]
        s = dot(k_ref[...], q, NT) * scale + bias[width:, :]
        p = jnp.exp2(s - st_ref[h, 0:1, :])
        ds = p * (dot(v_ref[...], do, NT) - st_ref[h, 1:2, :])
        p = p.astype(BF16)
        ds = ds.astype(BF16)
        o = dot(vt[:, :width], p_ref[h], NN) + dot(vt[:, width:], p, NN)
        out_ref[:, hs] = o.T.astype(BF16)
        g = dot(kt[:, :width], ds_ref[h], NN) + dot(kt[:, width:], ds, NN)
        dq_ref[:, hs] = (g * factor).T.astype(BF16)
        x = dot(ds, q, NN)
        y = dot(p, do, NN)
        dk = x if h == 0 else dk + x
        dv = y if h == 0 else dv + y
    mine_ref[0:rows, :] = dk * factor
    mine_ref[rows:, :] = dv


def call(kernel, name, outs, scratch, vmem, flops, *args):
    vm = pl.BlockSpec(memory_space=pltpu.VMEM)
    moved = sum(math.prod(a.shape) * a.dtype.itemsize for a in args)
    return pl.pallas_call(
        kernel,
        out_shape=[jax.ShapeDtypeStruct(*o) for o in outs],
        in_specs=[vm] * len(args),
        out_specs=[vm] * len(outs),
        scratch_shapes=[pltpu.VMEM(*s) for s in scratch],
        compiler_params=pltpu.CompilerParams(vmem_limit_bytes=vmem << 20),
        cost_estimate=pl.CostEstimate(flops=flops, bytes_accessed=moved, transcendentals=0),
        name=name,
    )(*args)


def attention_grads(lens, q, do, k, v, far, first_of):
    rows, hd = k.shape
    heads = q.shape[1] // hd
    width = REACH * rows
    block = 2 * heads * rows * rows * hd
    qs, dos, bias, st = call(
        functools.partial(local_kernel, first_of=first_of),
        "local",
        [((heads, rows, hd), BF16)] * 2 + [((width + rows, rows), F32), ((heads, 3, rows), F32)],
        [], 16, 2 * block, lens.reshape(1, -1), q, do, k, v,
    )
    *back, p, ds, st2 = call(
        remote_kernel,
        "remote",
        [((2 * rows, hd), BF16)] * REACH + [((heads, width, rows), BF16)] * 2 + [((heads, 2, rows), F32)],
        [((width, hd), BF16)] * 2
        + [((width, rows), F32)] * 2
        + [((8, rows), F32)]
        + [((width, hd), F32)] * 2,
        24, 16 * block, qs, dos, bias, st, *far,
    )
    return back, lambda: call(
        own_kernel,
        "own",
        [(q.shape, BF16)] * 2 + [((2 * rows, hd), F32)],
        [((hd, width + rows), BF16)] * 2,
        24, 14 * block, qs, dos, bias, st2, p, ds, k, v, *far,
    )


def shifted(block, distance):
    count = lax.axis_size("ctx") * lax.axis_size("grp")
    route = [(i, (i + distance) % count) for i in range(count)]
    return lax.ppermute(block, ("ctx", "grp"), route)


def body(queries, key_rows, value_rows, out_grad, doc_lengths):
    rows, hd = key_rows.shape

    def first_of():
        return (lax.axis_index("ctx") * lax.axis_size("grp") + lax.axis_index("grp")) * rows

    packed = jnp.concatenate([key_rows, value_rows], axis=0)
    far = [shifted(packed, d) for d in range(REACH, 0, -1)]
    back, finish = attention_grads(
        doc_lengths, queries, out_grad, key_rows, value_rows, far, first_of
    )
    came = [shifted(back[REACH - d], -d) for d in range(REACH, 0, -1)]
    attended, query_grad, total = finish()
    for part in came:
        total = total + part.astype(F32)
    total = total.astype(BF16)
    return attended, query_grad, total[:rows], total[rows:]


def solution(mesh):
    split = P(("ctx", "grp"), None)
    return jax.shard_map(
        body, mesh=mesh, in_specs=(split,) * 4 + (P(),), out_specs=(split,) * 4, check_vma=False
    )
```

time: 47.2 us -> 41.7 us (0.88)
  waiting for transfers between devices: 6.99 us -> 0.02 us
  local copies, waits for them, and re-layouts: 3.65 us -> 6.79 us
  starting transfers between devices: 21.9 us -> 19.5 us
  Pallas kernels: 13.2 us -> 14.2 us
    ppermute x8, waiting for transfers between devices: 6.99 us -> 0.02 us  [shifted(): return lax.ppermute(block, ('ctx', 'grp'), route)]
    ppermute x8, starting transfers between devices: 21.9 us -> 19.5 us  [shifted(): return lax.ppermute(block, ('ctx', 'grp'), route)]
    unnamed x11 -> x15, local copies, waits for them, and re-layouts: 2.97 us -> 5.27 us
    pallas_call x1 -> x3, Pallas kernels: 13.2 us -> 14.2 us  [call(): pl.pallas_call(kernel, out_shape=[jax.ShapeDtypeStruct(*o) for o in outs]...]
    concatenate x1, local copies, waits for them, and re-layouts: 0.01 us -> 0.85 us  [body(): packed = jnp.concatenate([key_rows, value_rows], axis=0)]
  transfers between devices with their start and end apart: 8 -> 8, of which waited for: 4 -> 0; matrix products, arithmetic and copies ran while one was open for 0% -> 0% of each run, Pallas kernels for 0% -> 15%
where the time goes in v2:
time: 41.7 us; the launch traced here: 41.3 us
  starting transfers between devices  19.5 us (47%)
  Pallas kernels  14.2 us (34%)
  local copies, waits for them, and re-layouts  6.79 us (16%)
  between operations  0.72 us (2%)
    ppermute x8, starting transfers between devices, shifted(): return lax.ppermute(block, ('ctx', 'grp'), route)  19.5 us
    pallas_call x3, Pallas kernels, call(): pl.pallas_call(kernel, out_shape=[jax.ShapeDtypeStruct(*o) for o in outs]...  14.2 us
    unnamed x15, local copies, waits for them, and re-layouts  5.27 us
    concatenate x1, local copies, waits for them, and re-layouts, body(): packed = jnp.concatenate([key_rows, value_rows], axis=0)  0.85 us
  transfers between devices with their start and end apart: 8, of which 0 were waited for; matrix products, arithmetic and copies ran while one was open for 0% of the time, Pallas kernels for 15%

profile of v2, /device:TPU:1, one launch (start us, length us, event | category | flops | bytes accessed | tf_op | source)
XLA Modules:
  0.0 41.3 jit_solution(7816663631920453363)
XLA Ops:
  0.6 0.8 %constant_dynamic-update-slice_fusion.1 = bf16[512,128]{1,0:T(8,128)(2,1)S(1)} fusion(bf16[256,128]{1,0:T(8,128)(2,1)} %k_ref.3), kind=kLoop, calls=%fused_computation.2 | loop fusion | bytes 131072
  1.5 0.9 %constant_dynamic-update-slice_fusion = bf16[512,128]{1,0:T(8,128)(2,1)S(1)} fusion(bf16[512,128]{1,0:T(8,128)(2,1)S(1)} %constant_dynamic-update-slice_fusion.1, bf16[256,128]{1,0:T(8,128)(2,1)} %v_ref.3), kind=kLoop, calls=%fused_computation.1 | loop fusion | bytes 131072 | tf_op jit(solution)/shard_map/concatenate | solution.py:221
  2.3 2.1 %collective-permute-start.3 = (bf16[512,128]{1,0:T(8,128)(2,1)S(1)}, bf16[512,128]{1,0:T(8,128)(2,1)S(1)}, u32[]{:S(2)}, u32[]{:S(2)}) collective-permute-start(bf16[512,128]{1,0:T(8,128)(2,1)S(1)} %constant_dynamic-update-slice_fusion), channel_id=1, source_target_pairs={{0,1},{1,2},{2,3},{3,4},{4,5},{5,6},{6,7},{7,8},{8,9},{9,10},{10,1... | collective-permute-start | bytes 393224 | tf_op jit(solution)/shard_map/ppermute | solution.py:212
  4.5 2.5 %collective-permute-start.2 = (bf16[512,128]{1,0:T(8,128)(2,1)S(1)}, bf16[512,128]{1,0:T(8,128)(2,1)S(1)}, u32[]{:S(2)}, u32[]{:S(2)}) collective-permute-start(bf16[512,128]{1,0:T(8,128)(2,1)S(1)} %constant_dynamic-update-slice_fusion), channel_id=1, source_target_pairs={{0,2},{1,3},{2,4},{3,5},{4,6},{5,7},{6,8},{7,9},{8,10},{9,11},{10,... | collective-permute-start | bytes 393224 | tf_op jit(solution)/shard_map/ppermute | solution.py:212
  6.9 3.3 %collective-permute-start.1 = (bf16[512,128]{1,0:T(8,128)(2,1)S(1)}, bf16[512,128]{1,0:T(8,128)(2,1)S(1)}, u32[]{:S(2)}, u32[]{:S(2)}) collective-permute-start(bf16[512,128]{1,0:T(8,128)(2,1)S(1)} %constant_dynamic-update-slice_fusion), channel_id=1, source_target_pairs={{0,3},{1,4},{2,5},{3,6},{4,7},{5,8},{6,9},{7,10},{8,11},{9,12},{10... | collective-permute-start | bytes 393224 | tf_op jit(solution)/shard_map/ppermute | solution.py:212
  10.3 0.0 collective-permute-start
  10.3 0.0 copy-start
  10.3 0.8 %copy-done = bf16[256,128]{1,0:T(8,128)(2,1)S(1)} copy-done((bf16[256,128]{1,0:T(8,128)(2,1)S(1)}, bf16[256,128]{1,0:T(8,128)(2,1)}, u32[]{:S(2)}) %copy-start) | copy-done | bytes 65560
  11.1 0.0 copy-start.2
  11.1 0.8 %copy-done.2 = bf16[256,128]{1,0:T(8,128)(2,1)S(1)} copy-done((bf16[256,128]{1,0:T(8,128)(2,1)S(1)}, bf16[256,128]{1,0:T(8,128)(2,1)}, u32[]{:S(2)}) %copy-start.2) | copy-done | bytes 65560
  11.9 0.0 copy-start.4
  11.9 1.0 %copy-done.4 = bf16[256,1024]{1,0:T(8,128)(2,1)S(1)} copy-done((bf16[256,1024]{1,0:T(8,128)(2,1)S(1)}, bf16[256,1024]{1,0:T(8,128)(2,1)}, u32[]{:S(2)}) %copy-start.4) | copy-done | bytes 524312
  13.0 0.0 copy-start.5
  13.0 1.0 %copy-done.5 = bf16[256,1024]{1,0:T(8,128)(2,1)S(1)} copy-done((bf16[256,1024]{1,0:T(8,128)(2,1)S(1)}, bf16[256,1024]{1,0:T(8,128)(2,1)}, u32[]{:S(2)}) %copy-start.5) | copy-done | bytes 524312
  14.0 0.0 copy-start.6
  14.0 0.7 %copy-done.6 = s32[128]{0:T(128)S(1)} copy-done((s32[128]{0:T(128)S(1)}, s32[128]{0:T(128)}, u32[]{:S(2)}) %copy-start.6) | copy-done | bytes 536
  14.7 1.3 %local.1 = (bf16[8,256,128]{2,1,0:T(8,128)(2,1)S(1)}, bf16[8,256,128]{2,1,0:T(8,128)(2,1)S(1)}, f32[1280,256]{1,0:T(8,128)S(1)}, f32[8,3,256]{2,1,0:T(4,128)S(1)}) custom-call(s32[1,128]{1,0:T(1,128)S(1)} %bitcast.1, bf16[256,1024]{1,0:T(8,128)(2,1)S(1)} %copy-done.4, bf16[256,1024]{1,0:T(8,128)(2,1)S(1)} %copy-done.5, bf16[256,128]{1,0:T(8,128)(2,1)S(1)} %copy-done, ...), custom_call_target="tpu_custom_call" | custom-call | flops 268435456 | bytes 1180160 | tf_op jit(solution)/shard_map/local/pallas_call | solution.py:167
  15.9 0.0 copy-start.1
  15.9 0.0 copy-start.3
  16.0 0.0 collective-permute-done.3.refs_3_
  16.0 0.0 collective-permute-done.2.refs_2_
  16.0 0.0 collective-permute-done.1.refs_1_
  16.0 0.0 collective-permute-done.refs_0_
  16.0 8.1 %remote.1 = (bf16[512,128]{1,0:T(8,128)(2,1)S(1)}, bf16[512,128]{1,0:T(8,128)(2,1)S(1)}, bf16[512,128]{1,0:T(8,128)(2,1)S(1)}, bf16[512,128]{1,0:T(8,128)(2,1)S(...) custom-call(bf16[8,256,128]{2,1,0:T(8,128)(2,1)S(1)} %get-tuple-element.18.q_ref,, ...), custom_call_target="tpu_custom_call" | custom-call | flops 2147483648 | bytes 2908160 | tf_op jit(solution)/shard_map/remote/pallas_call | solution.py:167
  24.1 4.9 %collective-permute-start.4 = (bf16[512,128]{1,0:T(8,128)(2,1)S(1)}, bf16[512,128]{1,0:T(8,128)(2,1)S(1)}, u32[]{:S(2)}, u32[]{:S(2)}) collective-permute-start(bf16[512,128]{1,0:T(8,128)(2,1)S(1)} %get-tuple-element.28), channel_id=1, source_target_pairs={{0,252},{1,253},{2,254},{3,255},{4,0},{5,1},{6,2},{7,3},{8,4},{9,5... | collective-permute-start | bytes 393224 | tf_op jit(solution)/shard_map/ppermute | solution.py:212
  29.0 2.5 %collective-permute-start.5 = (bf16[512,128]{1,0:T(8,128)(2,1)S(1)}, bf16[512,128]{1,0:T(8,128)(2,1)S(1)}, u32[]{:S(2)}, u32[]{:S(2)}) collective-permute-start(bf16[512,128]{1,0:T(8,128)(2,1)S(1)} %get-tuple-element.29), channel_id=1, source_target_pairs={{0,253},{1,254},{2,255},{3,0},{4,1},{5,2},{6,3},{7,4},{8,5},{9,6},... | collective-permute-start | bytes 393224 | tf_op jit(solution)/shard_map/ppermute | solution.py:212
  31.5 2.4 %collective-permute-start.6 = (bf16[512,128]{1,0:T(8,128)(2,1)S(1)}, bf16[512,128]{1,0:T(8,128)(2,1)S(1)}, u32[]{:S(2)}, u32[]{:S(2)}) collective-permute-start(bf16[512,128]{1,0:T(8,128)(2,1)S(1)} %get-tuple-element.30), channel_id=1, source_target_pairs={{0,254},{1,255},{2,0},{3,1},{4,2},{5,3},{6,4},{7,5},{8,6},{9,7},{1... | collective-permute-start | bytes 393224 | tf_op jit(solution)/shard_map/ppermute | solution.py:212
  34.0 1.7 %collective-permute-start.7 = (bf16[512,128]{1,0:T(8,128)(2,1)S(1)}, bf16[512,128]{1,0:T(8,128)(2,1)S(1)}, u32[]{:S(2)}, u32[]{:S(2)}) collective-permute-start(bf16[512,128]{1,0:T(8,128)(2,1)S(1)} %get-tuple-element.31), channel_id=1, source_target_pairs={{0,255},{1,0},{2,1},{3,2},{4,3},{5,4},{6,5},{7,6},{8,7},{9,8},{10,... | collective-permute-start | bytes 393224 | tf_op jit(solution)/shard_map/ppermute | solution.py:212
  35.7 0.0 copy-done.1
  35.7 0.0 copy-done.3
  35.7 4.8 %own.1 = (bf16[256,1024]{1,0:T(8,128)(2,1)}, bf16[256,1024]{1,0:T(8,128)(2,1)}, f32[512,128]{1,0:T(8,128)S(1)}) custom-call(bf16[8,256,128]{2,1,0:T(8,128)(2,1)S(1)} %get-tuple-element.18.q_ref, bf16[8,256,128]{2,1,0:T(8,128)(2,1)S(1)} %get-tuple-element.19.do_ref, f32[1280,256]{1,0:T(8,128)S(1)} %get-tuple-element.20.bias, ...), custom_call_target="tpu_custom_call" | custom-call | flops 1879048192 | bytes 11419648 | tf_op jit(solution)/shard_map/own/pallas_call | solution.py:167
  40.5 0.0 collective-permute-done.4
  40.5 0.0 collective-permute-done.5
  40.5 0.0 collective-permute-done.6
  40.5 0.0 collective-permute-done.7
  40.5 0.1 add_convert_fusion
  40.6 0.7 %fusion = (bf16[256,128]{1,0:T(8,128)(2,1)}, bf16[256,128]{1,0:T(8,128)(2,1)}) fusion(bf16[512,128]{1,0:T(8,128)(2,1)S(1)} %add_convert_fusion), kind=kLoop, calls=%fused_computation.3 | loop fusion | bytes 262144 | tf_op jit(solution)/shard_map/slice | solution.py:231
Async XLA Ops:
  2.3 13.6 %collective-permute-start.3 = (bf16[512,128]{1,0:T(8,128)(2,1)S(1)}, bf16[512,128]{1,0:T(8,128)(2,1)S(1)}, u32[]{:S(2)}, u32[]{:S(2)}) collective-permute-start(bf16[512,128]{1,0:T(8,128)(2,1)S(1)} %constant_dynamic-update-slice_fusion), channel_id=1, source_target_pairs={{0,1},{1,2},{2,3},{3,4},{4,5},{5,6},{6,7},{7,8},{8,9},{9,10},{10,1... | collective-permute-start | bytes 393224 | tf_op jit(solution)/shard_map/ppermute | solution.py:212
  4.5 11.5 %collective-permute-start.2 = (bf16[512,128]{1,0:T(8,128)(2,1)S(1)}, bf16[512,128]{1,0:T(8,128)(2,1)S(1)}, u32[]{:S(2)}, u32[]{:S(2)}) collective-permute-start(bf16[512,128]{1,0:T(8,128)(2,1)S(1)} %constant_dynamic-update-slice_fusion), channel_id=1, source_target_pairs={{0,2},{1,3},{2,4},{3,5},{4,6},{5,7},{6,8},{7,9},{8,10},{9,11},{10,... | collective-permute-start | bytes 393224 | tf_op jit(solution)/shard_map/ppermute | solution.py:212
  6.9 9.1 %collective-permute-start.1 = (bf16[512,128]{1,0:T(8,128)(2,1)S(1)}, bf16[512,128]{1,0:T(8,128)(2,1)S(1)}, u32[]{:S(2)}, u32[]{:S(2)}) collective-permute-start(bf16[512,128]{1,0:T(8,128)(2,1)S(1)} %constant_dynamic-update-slice_fusion), channel_id=1, source_target_pairs={{0,3},{1,4},{2,5},{3,6},{4,7},{5,8},{6,9},{7,10},{8,11},{9,12},{10... | collective-permute-start | bytes 393224 | tf_op jit(solution)/shard_map/ppermute | solution.py:212
  10.3 5.7 %collective-permute-start = (bf16[512,128]{1,0:T(8,128)(2,1)S(1)}, bf16[512,128]{1,0:T(8,128)(2,1)S(1)}, u32[]{:S(2)}, u32[]{:S(2)}) collective-permute-start(bf16[512,128]{1,0:T(8,128)(2,1)S(1)} %constant_dynamic-update-slice_fusion), channel_id=1, source_target_pairs={{0,4},{1,5},{2,6},{3,7},{4,8},{5,9},{6,10},{7,11},{8,12},{9,13},{1... | collective-permute-start | bytes 393224 | tf_op jit(solution)/shard_map/ppermute | solution.py:212
  10.3 0.8 %copy-start = (bf16[256,128]{1,0:T(8,128)(2,1)S(1)}, bf16[256,128]{1,0:T(8,128)(2,1)}, u32[]{:S(2)}) copy-start(bf16[256,128]{1,0:T(8,128)(2,1)} %k_ref.3) | copy-start | bytes 196612
  11.1 0.8 %copy-start.2 = (bf16[256,128]{1,0:T(8,128)(2,1)S(1)}, bf16[256,128]{1,0:T(8,128)(2,1)}, u32[]{:S(2)}) copy-start(bf16[256,128]{1,0:T(8,128)(2,1)} %v_ref.3) | copy-start | bytes 196612
  11.9 1.0 %copy-start.4 = (bf16[256,1024]{1,0:T(8,128)(2,1)S(1)}, bf16[256,1024]{1,0:T(8,128)(2,1)}, u32[]{:S(2)}) copy-start(bf16[256,1024]{1,0:T(8,128)(2,1)} %q_ref.1) | copy-start | bytes 1572868
  13.0 1.0 %copy-start.5 = (bf16[256,1024]{1,0:T(8,128)(2,1)S(1)}, bf16[256,1024]{1,0:T(8,128)(2,1)}, u32[]{:S(2)}) copy-start(bf16[256,1024]{1,0:T(8,128)(2,1)} %do_ref.1) | copy-start | bytes 1572868
  14.0 0.7 %copy-start.6 = (s32[128]{0:T(128)S(1)}, s32[128]{0:T(128)}, u32[]{:S(2)}) copy-start(s32[128]{0:T(128)} %param.9) | copy-start | bytes 1540
  15.9 19.7 %copy-start.1 = (bf16[256,128]{1,0:T(8,128)(2,1)S(1)}, bf16[256,128]{1,0:T(8,128)(2,1)}, u32[]{:S(2)}) copy-start(bf16[256,128]{1,0:T(8,128)(2,1)} %k_ref.3) | copy-start | bytes 196612
  15.9 19.7 %copy-start.3 = (bf16[256,128]{1,0:T(8,128)(2,1)S(1)}, bf16[256,128]{1,0:T(8,128)(2,1)}, u32[]{:S(2)}) copy-start(bf16[256,128]{1,0:T(8,128)(2,1)} %v_ref.3) | copy-start | bytes 196612
  24.1 16.4 %collective-permute-start.4 = (bf16[512,128]{1,0:T(8,128)(2,1)S(1)}, bf16[512,128]{1,0:T(8,128)(2,1)S(1)}, u32[]{:S(2)}, u32[]{:S(2)}) collective-permute-start(bf16[512,128]{1,0:T(8,128)(2,1)S(1)} %get-tuple-element.28), channel_id=1, source_target_pairs={{0,252},{1,253},{2,254},{3,255},{4,0},{5,1},{6,2},{7,3},{8,4},{9,5... | collective-permute-start | bytes 393224 | tf_op jit(solution)/shard_map/ppermute | solution.py:212
  29.0 11.5 %collective-permute-start.5 = (bf16[512,128]{1,0:T(8,128)(2,1)S(1)}, bf16[512,128]{1,0:T(8,128)(2,1)S(1)}, u32[]{:S(2)}, u32[]{:S(2)}) collective-permute-start(bf16[512,128]{1,0:T(8,128)(2,1)S(1)} %get-tuple-element.29), channel_id=1, source_target_pairs={{0,253},{1,254},{2,255},{3,0},{4,1},{5,2},{6,3},{7,4},{8,5},{9,6},... | collective-permute-start | bytes 393224 | tf_op jit(solution)/shard_map/ppermute | solution.py:212
  31.5 9.0 %collective-permute-start.6 = (bf16[512,128]{1,0:T(8,128)(2,1)S(1)}, bf16[512,128]{1,0:T(8,128)(2,1)S(1)}, u32[]{:S(2)}, u32[]{:S(2)}) collective-permute-start(bf16[512,128]{1,0:T(8,128)(2,1)S(1)} %get-tuple-element.30), channel_id=1, source_target_pairs={{0,254},{1,255},{2,0},{3,1},{4,2},{5,3},{6,4},{7,5},{8,6},{9,7},{1... | collective-permute-start | bytes 393224 | tf_op jit(solution)/shard_map/ppermute | solution.py:212
  34.0 6.6 %collective-permute-start.7 = (bf16[512,128]{1,0:T(8,128)(2,1)S(1)}, bf16[512,128]{1,0:T(8,128)(2,1)S(1)}, u32[]{:S(2)}, u32[]{:S(2)}) collective-permute-start(bf16[512,128]{1,0:T(8,128)(2,1)S(1)} %get-tuple-element.31), channel_id=1, source_target_pairs={{0,255},{1,0},{2,1},{3,2},{4,3},{5,4},{6,5},{7,6},{8,7},{9,8},{10,... | collective-permute-start | bytes 393224 | tf_op jit(solution)/shard_map/ppermute | solution.py:212

commit v3 on v2

--- a/solution.py
+++ b/solution.py
@@ -14,6 +14,7 @@
 LOG2E = 1.4426950408889634
 REACH = 4
 CHUNK = 64
+STAGE_MB = 16
 
 
 def dot(a, b, dims):
@@ -24,7 +25,23 @@
     return op(x.reshape(x.shape[0] // 8, 8, x.shape[1]), axis=0)
 
 
-def local_kernel(lens_ref, q_ref, do_ref, k_ref, v_ref, qs, dos, bias, st_ref, *, first_of):
+def stage_kernel(k_hbm, v_hbm, q_hbm, do_hbm, lens_hbm, packed, q, do, lens, sem):
+    rows = k_hbm.shape[0]
+    pairs = (
+        (k_hbm, packed.at[0:rows, :]),
+        (v_hbm, packed.at[rows : 2 * rows, :]),
+        (q_hbm, q),
+        (do_hbm, do),
+        (lens_hbm, lens),
+    )
+    copies = [pltpu.make_async_copy(a, b, sem.at[i]) for i, (a, b) in enumerate(pairs)]
+    for c in copies:
+        c.start()
+    for c in copies:
+        c.wait()
+
+
+def local_kernel(lens_ref, q_ref, do_ref, kv_ref, qs, dos, bias, st_ref, *, first_of):
     heads, rows, hd = qs.shape
     scale = LOG2E / math.sqrt(hd)
     q0 = first_of()
@@ -46,10 +63,10 @@
         do = do_ref[:, h * hd : (h + 1) * hd]
         qs[h] = q
         dos[h] = do
-        s = dot(k_ref[...], q, NT) * scale + bias[REACH * rows :, :]
+        s = dot(kv_ref[0:rows, :], q, NT) * scale + bias[REACH * rows :, :]
         m = jnp.max(fold(s, jnp.max), axis=0, keepdims=True)
         p = jnp.exp2(s - m)
-        dp = dot(v_ref[...], do, NT)
+        dp = dot(kv_ref[rows:, :], do, NT)
         st_ref[h, 0:1, :] = m
         st_ref[h, 1:2, :] = jnp.sum(fold(p, jnp.sum), axis=0, keepdims=True)
         st_ref[h, 2:3, :] = jnp.sum(fold(p * dp, jnp.sum), axis=0, keepdims=True)
@@ -127,7 +144,7 @@
         back[b][rows:, :] = dv_acc[bs, :].astype(BF16)
 
 
-def own_kernel(q_ref, do_ref, bias, st_ref, p_ref, ds_ref, k_ref, v_ref, *refs):
+def own_kernel(q_ref, do_ref, bias, st_ref, p_ref, ds_ref, kv_ref, *refs):
     far = refs[:REACH]
     out_ref, dq_ref, mine_ref, kt, vt = refs[REACH:]
     heads, rows, hd = q_ref.shape
@@ -137,16 +154,18 @@
     for b in range(REACH):
         kt[:, b * rows : (b + 1) * rows] = far[b][0:rows, :].T
         vt[:, b * rows : (b + 1) * rows] = far[b][rows:, :].T
-    kt[:, width:] = k_ref[...].T
-    vt[:, width:] = v_ref[...].T
+    k = kv_ref[0:rows, :]
+    v = kv_ref[rows:, :]
+    kt[:, width:] = k.T
+    vt[:, width:] = v.T
     dk = dv = None
     for h in range(heads):
         hs = slice(h * hd, (h + 1) * hd)
         q = q_ref[h]
         do = do_ref[h]
-        s = dot(k_ref[...], q, NT) * scale + bias[width:, :]
+        s = dot(k, q, NT) * scale + bias[width:, :]
         p = jnp.exp2(s - st_ref[h, 0:1, :])
-        ds = p * (dot(v_ref[...], do, NT) - st_ref[h, 1:2, :])
+        ds = p * (dot(v, do, NT) - st_ref[h, 1:2, :])
         p = p.astype(BF16)
         ds = ds.astype(BF16)
         o = dot(vt[:, :width], p_ref[h], NN) + dot(vt[:, width:], p, NN)
@@ -161,23 +180,34 @@
     mine_ref[rows:, :] = dv
 
 
-def call(kernel, name, outs, scratch, vmem, flops, *args):
+def call(kernel, name, outs, scratch, vmem, flops, *args, in_hbm=0):
     vm = pl.BlockSpec(memory_space=pltpu.VMEM)
+    hbm = pl.BlockSpec(memory_space=pltpu.HBM)
     moved = sum(math.prod(a.shape) * a.dtype.itemsize for a in args)
     return pl.pallas_call(
         kernel,
         out_shape=[jax.ShapeDtypeStruct(*o) for o in outs],
-        in_specs=[vm] * len(args),
+        in_specs=[hbm] * in_hbm + [vm] * (len(args) - in_hbm),
         out_specs=[vm] * len(outs),
-        scratch_shapes=[pltpu.VMEM(*s) for s in scratch],
-        compiler_params=pltpu.CompilerParams(vmem_limit_bytes=vmem << 20),
+        scratch_shapes=[pltpu.VMEM(*s) if isinstance(s, tuple) else s for s in scratch],
+        compiler_params=pltpu.CompilerParams(vmem_limit_bytes=int(vmem * 2**20)),
         cost_estimate=pl.CostEstimate(flops=flops, bytes_accessed=moved, transcendentals=0),
         name=name,
-    )(*args)
-
-
-def attention_grads(lens, q, do, k, v, far, first_of):
+    )(*(pltpu.with_memory_space_constraint(a, pltpu.HBM) for a in args[:in_hbm]), *args[in_hbm:])
+
+
+def stage(k, v, q, do, lens):
     rows, hd = k.shape
+    return call(
+        stage_kernel,
+        "stage",
+        [((2 * rows, hd), BF16), (q.shape, BF16), (do.shape, BF16), ((1, lens.shape[0]), jnp.int32)],
+        [pltpu.SemaphoreType.DMA((5,))], STAGE_MB, 0, k, v, q, do, lens.reshape(1, -1), in_hbm=5,
+    )
+
+
+def attention_grads(lens, q, do, packed, far, first_of):
+    rows, hd = packed.shape[0] // 2, packed.shape[1]
     heads = q.shape[1] // hd
     width = REACH * rows
     block = 2 * heads * rows * rows * hd
@@ -185,7 +215,7 @@
         functools.partial(local_kernel, first_of=first_of),
         "local",
         [((heads, rows, hd), BF16)] * 2 + [((width + rows, rows), F32), ((heads, 3, rows), F32)],
-        [], 16, 2 * block, lens.reshape(1, -1), q, do, k, v,
+        [], 16, 2 * block, lens, q, do, packed,
     )
     *back, p, ds, st2 = call(
         remote_kernel,
@@ -202,7 +232,7 @@
         "own",
         [(q.shape, BF16)] * 2 + [((2 * rows, hd), F32)],
         [((hd, width + rows), BF16)] * 2,
-        24, 14 * block, qs, dos, bias, st2, p, ds, k, v, *far,
+        24, 14 * block, qs, dos, bias, st2, p, ds, packed, *far,
     )
 
 
@@ -218,10 +248,10 @@
     def first_of():
         return (lax.axis_index("ctx") * lax.axis_size("grp") + lax.axis_index("grp")) * rows
 
-    packed = jnp.concatenate([key_rows, value_rows], axis=0)
+    packed, q, do, lens = stage(key_rows, value_rows, queries, out_grad, doc_lengths)
     far = [shifted(packed, d) for d in range(REACH, 0, -1)]
     back, finish = attention_grads(
-        doc_lengths, queries, out_grad, key_rows, value_rows, far, first_of
+        lens, q, do, packed, far, first_of
     )
     came = [shifted(back[REACH - d], -d) for d in range(REACH, 0, -1)]
     attended, query_grad, total = finish()

time: 41.7 us -> 41 us (0.983)
  local copies, waits for them, and re-layouts: 6.79 us -> 0.66 us
  starting transfers between devices: 19.5 us -> 22.1 us
  waiting for transfers between devices: 0.02 us -> 1.93 us
  Pallas kernels: 14.2 us -> 15.4 us
    unnamed x15 -> x0, local copies, waits for them, and re-layouts: 5.27 us -> none
    ppermute x8, starting transfers between devices: 19.5 us -> 22.1 us  [shifted(): return lax.ppermute(block, ('ctx', 'grp'), route)]
    ppermute x8, waiting for transfers between devices: 0.02 us -> 1.93 us  [shifted(): return lax.ppermute(block, ('ctx', 'grp'), route)]
    pallas_call x3 -> x4, Pallas kernels: 14.2 us -> 15.4 us  [call(): pl.pallas_call(kernel, out_shape=[jax.ShapeDtypeStruct(*o) for o in outs]...]
    concatenate x1 -> x0, local copies, waits for them, and re-layouts: 0.85 us -> none  [body(): packed = jnp.concatenate([key_rows, value_rows], axis=0)]
  transfers between devices with their start and end apart: 8 -> 8, of which waited for: 0 -> 2; matrix products, arithmetic and copies ran while one was open for 0% -> 0% of each run, Pallas kernels for 15% -> 15%
where the time goes in v3:
time: 41 us; the launch traced here: 40.9 us
  starting transfers between devices  22.1 us (54%)
  Pallas kernels  15.4 us (38%)
  waiting for transfers between devices  1.93 us (5%)
  between operations  0.69 us (2%)
  local copies, waits for them, and re-layouts  0.66 us (2%)
    ppermute x8, starting transfers between devices, shifted(): return lax.ppermute(block, ('ctx', 'grp'), route)  22.1 us
    pallas_call x4, Pallas kernels, call(): pl.pallas_call(kernel, out_shape=[jax.ShapeDtypeStruct(*o) for o in outs]...  15.4 us
    ppermute x8, waiting for transfers between devices, shifted(): return lax.ppermute(block, ('ctx', 'grp'), route)  1.93 us
  transfers between devices with their start and end apart: 8, of which 2 were waited for; matrix products, arithmetic and copies ran while one was open for 0% of the time, Pallas kernels for 15%

profile of v3, /device:TPU:1, one launch (start us, length us, event | category | flops | bytes accessed | tf_op | source)
XLA Modules:
  0.0 40.9 jit_solution(18046684592470302553)
XLA Ops:
  0.6 1.3 %stage.1 = (bf16[512,128]{1,0:T(8,128)(2,1)S(1)}, bf16[256,1024]{1,0:T(8,128)(2,1)S(1)}, bf16[256,1024]{1,0:T(8,128)(2,1)S(1)}, s32[1,128]{1,0:T(1,128)S(1)}) custom-call(bf16[256,128]{1,0:T(8,128)(2,1)} %k_hbm.1, bf16[256,128]{1,0:T(8,128)(2,1)} %v_hbm.1, bf16[256,1024]{1,0:T(8,128)(2,1)} %q_hbm.1, bf16[256,1024]{1,0:T(8,128)(2,1)} %do_hbm.1, s32[1,128]{1,0:T(1,128)} %bitcast.1), custom_call_target="tpu_custom_call" | custom-call | bytes 1180160 | tf_op jit(solution)/shard_map/stage/pallas_call | solution.py:187
  2.0 2.1 %collective-permute-start.3 = (bf16[512,128]{1,0:T(8,128)(2,1)S(1)}, bf16[512,128]{1,0:T(8,128)(2,1)S(1)}, u32[]{:S(2)}, u32[]{:S(2)}) collective-permute-start(bf16[512,128]{1,0:T(8,128)(2,1)S(1)} %get-tuple-element.25.kv_ref), channel_id=1, source_target_pairs={{0,1},{1,2},{2,3},{3,4},{4,5},{5,6},{6,7},{7,8},{8,9},{9,10},{10,1... | collective-permute-start | bytes 393224 | tf_op jit(solution)/shard_map/ppermute | solution.py:242
  4.1 2.5 %collective-permute-start.2 = (bf16[512,128]{1,0:T(8,128)(2,1)S(1)}, bf16[512,128]{1,0:T(8,128)(2,1)S(1)}, u32[]{:S(2)}, u32[]{:S(2)}) collective-permute-start(bf16[512,128]{1,0:T(8,128)(2,1)S(1)} %get-tuple-element.25.kv_ref), channel_id=1, source_target_pairs={{0,2},{1,3},{2,4},{3,5},{4,6},{5,7},{6,8},{7,9},{8,10},{9,11},{10,... | collective-permute-start | bytes 393224 | tf_op jit(solution)/shard_map/ppermute | solution.py:242
  6.5 3.3 %collective-permute-start.1 = (bf16[512,128]{1,0:T(8,128)(2,1)S(1)}, bf16[512,128]{1,0:T(8,128)(2,1)S(1)}, u32[]{:S(2)}, u32[]{:S(2)}) collective-permute-start(bf16[512,128]{1,0:T(8,128)(2,1)S(1)} %get-tuple-element.25.kv_ref), channel_id=1, source_target_pairs={{0,3},{1,4},{2,5},{3,6},{4,7},{5,8},{6,9},{7,10},{8,11},{9,12},{10... | collective-permute-start | bytes 393224 | tf_op jit(solution)/shard_map/ppermute | solution.py:242
  9.9 0.0 collective-permute-start
  9.9 1.2 %local.1 = (bf16[8,256,128]{2,1,0:T(8,128)(2,1)S(1)}, bf16[8,256,128]{2,1,0:T(8,128)(2,1)S(1)}, f32[1280,256]{1,0:T(8,128)S(1)}, f32[8,3,256]{2,1,0:T(4,128)S(1)}) custom-call(s32[1,128]{1,0:T(1,128)S(1)} %get-tuple-element.22.lens_ref, bf16[256,1024]{1,0:T(8,128)(2,1)S(1)} %get-tuple-element.23.q_ref, bf16[256,1024]{1,0:T(8,128)(2,1)S(1)} %get-tuple-element.24.do_ref, ...), custom_call_target="tpu_custom_call" | custom-call | flops 268435456 | bytes 1180160 | tf_op jit(solution)/shard_map/local/pallas_call | solution.py:187
  11.1 0.0 collective-permute-done.3.refs_3_
  11.1 0.7 %collective-permute-done.2.refs_2_ = bf16[512,128]{1,0:T(8,128)(2,1)S(1)} collective-permute-done((bf16[512,128]{1,0:T(8,128)(2,1)S(1)}, bf16[512,128]{1,0:T(8,128)(2,1)S(1)}, u32[]{:S(2)}, u32[]{:S(2)}) %collective-permute-start.2) | collective-permute-done | bytes 131104 | tf_op jit(solution)/shard_map/ppermute | solution.py:242
  11.8 1.2 %collective-permute-done.1.refs_1_ = bf16[512,128]{1,0:T(8,128)(2,1)S(1)} collective-permute-done((bf16[512,128]{1,0:T(8,128)(2,1)S(1)}, bf16[512,128]{1,0:T(8,128)(2,1)S(1)}, u32[]{:S(2)}, u32[]{:S(2)}) %collective-permute-start.1) | collective-permute-done | bytes 131104 | tf_op jit(solution)/shard_map/ppermute | solution.py:242
  13.0 0.0 collective-permute-done.refs_0_
  13.0 8.1 %remote.1 = (bf16[512,128]{1,0:T(8,128)(2,1)S(1)}, bf16[512,128]{1,0:T(8,128)(2,1)S(1)}, bf16[512,128]{1,0:T(8,128)(2,1)S(1)}, bf16[512,128]{1,0:T(8,128)(2,1)S(...) custom-call(bf16[8,256,128]{2,1,0:T(8,128)(2,1)S(1)} %get-tuple-element.26.q_ref,, ...), custom_call_target="tpu_custom_call" | custom-call | flops 2147483648 | bytes 2908160 | tf_op jit(solution)/shard_map/remote/pallas_call | solution.py:187
  21.1 7.5 %collective-permute-start.4 = (bf16[512,128]{1,0:T(8,128)(2,1)S(1)}, bf16[512,128]{1,0:T(8,128)(2,1)S(1)}, u32[]{:S(2)}, u32[]{:S(2)}) collective-permute-start(bf16[512,128]{1,0:T(8,128)(2,1)S(1)} %get-tuple-element.36), channel_id=1, source_target_pairs={{0,252},{1,253},{2,254},{3,255},{4,0},{5,1},{6,2},{7,3},{8,4},{9,5... | collective-permute-start | bytes 393224 | tf_op jit(solution)/shard_map/ppermute | solution.py:242
  28.7 2.5 %collective-permute-start.5 = (bf16[512,128]{1,0:T(8,128)(2,1)S(1)}, bf16[512,128]{1,0:T(8,128)(2,1)S(1)}, u32[]{:S(2)}, u32[]{:S(2)}) collective-permute-start(bf16[512,128]{1,0:T(8,128)(2,1)S(1)} %get-tuple-element.37), channel_id=1, source_target_pairs={{0,253},{1,254},{2,255},{3,0},{4,1},{5,2},{6,3},{7,4},{8,5},{9,6},... | collective-permute-start | bytes 393224 | tf_op jit(solution)/shard_map/ppermute | solution.py:242
  31.1 2.4 %collective-permute-start.6 = (bf16[512,128]{1,0:T(8,128)(2,1)S(1)}, bf16[512,128]{1,0:T(8,128)(2,1)S(1)}, u32[]{:S(2)}, u32[]{:S(2)}) collective-permute-start(bf16[512,128]{1,0:T(8,128)(2,1)S(1)} %get-tuple-element.38), channel_id=1, source_target_pairs={{0,254},{1,255},{2,0},{3,1},{4,2},{5,3},{6,4},{7,5},{8,6},{9,7},{1... | collective-permute-start | bytes 393224 | tf_op jit(solution)/shard_map/ppermute | solution.py:242
  33.6 1.7 %collective-permute-start.7 = (bf16[512,128]{1,0:T(8,128)(2,1)S(1)}, bf16[512,128]{1,0:T(8,128)(2,1)S(1)}, u32[]{:S(2)}, u32[]{:S(2)}) collective-permute-start(bf16[512,128]{1,0:T(8,128)(2,1)S(1)} %get-tuple-element.39), channel_id=1, source_target_pairs={{0,255},{1,0},{2,1},{3,2},{4,3},{5,4},{6,5},{7,6},{8,7},{9,8},{10,... | collective-permute-start | bytes 393224 | tf_op jit(solution)/shard_map/ppermute | solution.py:242
  35.3 4.8 %own.1 = (bf16[256,1024]{1,0:T(8,128)(2,1)}, bf16[256,1024]{1,0:T(8,128)(2,1)}, f32[512,128]{1,0:T(8,128)S(1)}) custom-call(bf16[8,256,128]{2,1,0:T(8,128)(2,1)S(1)} %get-tuple-element.26.q_ref, bf16[8,256,128]{2,1,0:T(8,128)(2,1)S(1)} %get-tuple-element.27.do_ref, f32[1280,256]{1,0:T(8,128)S(1)} %get-tuple-element.28.bias, ...), custom_call_target="tpu_custom_call" | custom-call | flops 1879048192 | bytes 11419648 | tf_op jit(solution)/shard_map/own/pallas_call | solution.py:187
  40.1 0.0 collective-permute-done.4
  40.1 0.0 collective-permute-done.5
  40.1 0.0 collective-permute-done.6
  40.1 0.0 collective-permute-done.7
  40.1 0.1 add_convert_fusion
  40.2 0.7 %fusion = (bf16[256,128]{1,0:T(8,128)(2,1)}, bf16[256,128]{1,0:T(8,128)(2,1)}) fusion(bf16[512,128]{1,0:T(8,128)(2,1)S(1)} %add_convert_fusion), kind=kLoop, calls=%fused_computation.1 | loop fusion | bytes 262144 | tf_op jit(solution)/shard_map/slice | solution.py:261
Async XLA Ops:
  2.0 9.1 %collective-permute-start.3 = (bf16[512,128]{1,0:T(8,128)(2,1)S(1)}, bf16[512,128]{1,0:T(8,128)(2,1)S(1)}, u32[]{:S(2)}, u32[]{:S(2)}) collective-permute-start(bf16[512,128]{1,0:T(8,128)(2,1)S(1)} %get-tuple-element.25.kv_ref), channel_id=1, source_target_pairs={{0,1},{1,2},{2,3},{3,4},{4,5},{5,6},{6,7},{7,8},{8,9},{9,10},{10,1... | collective-permute-start | bytes 393224 | tf_op jit(solution)/shard_map/ppermute | solution.py:242
  4.1 7.7 %collective-permute-start.2 = (bf16[512,128]{1,0:T(8,128)(2,1)S(1)}, bf16[512,128]{1,0:T(8,128)(2,1)S(1)}, u32[]{:S(2)}, u32[]{:S(2)}) collective-permute-start(bf16[512,128]{1,0:T(8,128)(2,1)S(1)} %get-tuple-element.25.kv_ref), channel_id=1, source_target_pairs={{0,2},{1,3},{2,4},{3,5},{4,6},{5,7},{6,8},{7,9},{8,10},{9,11},{10,... | collective-permute-start | bytes 393224 | tf_op jit(solution)/shard_map/ppermute | solution.py:242
  6.5 6.5 %collective-permute-start.1 = (bf16[512,128]{1,0:T(8,128)(2,1)S(1)}, bf16[512,128]{1,0:T(8,128)(2,1)S(1)}, u32[]{:S(2)}, u32[]{:S(2)}) collective-permute-start(bf16[512,128]{1,0:T(8,128)(2,1)S(1)} %get-tuple-element.25.kv_ref), channel_id=1, source_target_pairs={{0,3},{1,4},{2,5},{3,6},{4,7},{5,8},{6,9},{7,10},{8,11},{9,12},{10... | collective-permute-start | bytes 393224 | tf_op jit(solution)/shard_map/ppermute | solution.py:242
  9.9 3.1 %collective-permute-start = (bf16[512,128]{1,0:T(8,128)(2,1)S(1)}, bf16[512,128]{1,0:T(8,128)(2,1)S(1)}, u32[]{:S(2)}, u32[]{:S(2)}) collective-permute-start(bf16[512,128]{1,0:T(8,128)(2,1)S(1)} %get-tuple-element.25.kv_ref), channel_id=1, source_target_pairs={{0,4},{1,5},{2,6},{3,7},{4,8},{5,9},{6,10},{7,11},{8,12},{9,13},{1... | collective-permute-start | bytes 393224 | tf_op jit(solution)/shard_map/ppermute | solution.py:242
  21.1 19.0 %collective-permute-start.4 = (bf16[512,128]{1,0:T(8,128)(2,1)S(1)}, bf16[512,128]{1,0:T(8,128)(2,1)S(1)}, u32[]{:S(2)}, u32[]{:S(2)}) collective-permute-start(bf16[512,128]{1,0:T(8,128)(2,1)S(1)} %get-tuple-element.36), channel_id=1, source_target_pairs={{0,252},{1,253},{2,254},{3,255},{4,0},{5,1},{6,2},{7,3},{8,4},{9,5... | collective-permute-start | bytes 393224 | tf_op jit(solution)/shard_map/ppermute | solution.py:242
  28.7 11.5 %collective-permute-start.5 = (bf16[512,128]{1,0:T(8,128)(2,1)S(1)}, bf16[512,128]{1,0:T(8,128)(2,1)S(1)}, u32[]{:S(2)}, u32[]{:S(2)}) collective-permute-start(bf16[512,128]{1,0:T(8,128)(2,1)S(1)} %get-tuple-element.37), channel_id=1, source_target_pairs={{0,253},{1,254},{2,255},{3,0},{4,1},{5,2},{6,3},{7,4},{8,5},{9,6},... | collective-permute-start | bytes 393224 | tf_op jit(solution)/shard_map/ppermute | solution.py:242
  31.1 9.0 %collective-permute-start.6 = (bf16[512,128]{1,0:T(8,128)(2,1)S(1)}, bf16[512,128]{1,0:T(8,128)(2,1)S(1)}, u32[]{:S(2)}, u32[]{:S(2)}) collective-permute-start(bf16[512,128]{1,0:T(8,128)(2,1)S(1)} %get-tuple-element.38), channel_id=1, source_target_pairs={{0,254},{1,255},{2,0},{3,1},{4,2},{5,3},{6,4},{7,5},{8,6},{9,7},{1... | collective-permute-start | bytes 393224 | tf_op jit(solution)/shard_map/ppermute | solution.py:242
  33.6 6.5 %collective-permute-start.7 = (bf16[512,128]{1,0:T(8,128)(2,1)S(1)}, bf16[512,128]{1,0:T(8,128)(2,1)S(1)}, u32[]{:S(2)}, u32[]{:S(2)}) collective-permute-start(bf16[512,128]{1,0:T(8,128)(2,1)S(1)} %get-tuple-element.39), channel_id=1, source_target_pairs={{0,255},{1,0},{2,1},{3,2},{4,3},{5,4},{6,5},{7,6},{8,7},{9,8},{10,... | collective-permute-start | bytes 393224 | tf_op jit(solution)/shard_map/ppermute | solution.py:242

commit v4 on v3

v4 whole, which is shorter than its diff:
```python
import functools
import math

import jax
import jax.numpy as jnp
from jax import lax
from jax.experimental import pallas as pl
from jax.experimental.pallas import tpu as pltpu
from jax.sharding import PartitionSpec as P

F32, BF16 = jnp.float32, jnp.bfloat16
NT = (((1,), (1,)), ((), ()))
NN = (((1,), (0,)), ((), ()))
LOG2E = 1.4426950408889634
REACH = 4
CHUNK = 64
STAGE_MB = 16


def dot(a, b, dims):
    return lax.dot_general(a, b, dims, preferred_element_type=F32)


def fold(x, op):
    return op(x.reshape(x.shape[0] // 8, 8, x.shape[1]), axis=0)


def stage_kernel(k_hbm, v_hbm, packed, sem):
    rows = k_hbm.shape[0]
    copies = [
        pltpu.make_async_copy(k_hbm, packed.at[0:rows, :], sem.at[0]),
        pltpu.make_async_copy(v_hbm, packed.at[rows : 2 * rows, :], sem.at[1]),
    ]
    for c in copies:
        c.start()
    for c in copies:
        c.wait()


def local_kernel(
    lens_hbm, q_hbm, do_hbm, kv_ref, qs, dos, dot_t, reach_ref, s_own, dp_own, m_own, l_own, o_own,
    lens_ref, q_ref, do_ref, sem, *, first_of
):
    heads, rows, hd = qs.shape
    scale = LOG2E / math.sqrt(hd)
    copies = [
        pltpu.make_async_copy(src, dst, sem.at[i])
        for i, (src, dst) in enumerate(((lens_hbm, lens_ref), (q_hbm, q_ref), (do_hbm, do_ref)))
    ]
    for c in copies:
        c.start()
    copies[0].wait()
    q0 = first_of()
    nd = lens_ref.shape[1]
    lens = lens_ref[...]
    di = lax.broadcasted_iota(jnp.int32, (nd, nd), 0)
    dj = lax.broadcasted_iota(jnp.int32, (nd, nd), 1)
    ends = jnp.sum(jnp.where(dj <= di, lens, 0), axis=1, keepdims=True)
    length = jnp.sum(jnp.where(dj == di, lens, 0), axis=1, keepdims=True)
    qpos = lax.broadcasted_iota(jnp.int32, (1, rows), 1)
    begin = jnp.sum(jnp.where(ends <= qpos + q0, length, 0), axis=0, keepdims=True) - q0
    reach_ref[...] = begin
    kpos = lax.broadcasted_iota(jnp.int32, (rows, 1), 0)
    hide = jnp.where((kpos >= begin) & (kpos <= qpos), 0.0, -jnp.inf)
    vt = kv_ref[rows:, :].T
    copies[1].wait()
    copies[2].wait()
    for h in range(heads):
        q = q_ref[:, h * hd : (h + 1) * hd]
        do = do_ref[:, h * hd : (h + 1) * hd]
        qs[h] = q
        dos[h] = do
        dot_t[h] = do.T
        s = dot(kv_ref[0:rows, :], q, NT) * scale + hide
        m = jnp.max(fold(s, jnp.max), axis=0, keepdims=True)
        p = jnp.exp2(s - m)
        s_own[h] = s
        dp_own[h] = dot(kv_ref[rows:, :], do, NT).astype(BF16)
        m_own[h] = m
        l_own[h] = jnp.sum(fold(p, jnp.sum), axis=0, keepdims=True)
        o_own[h] = dot(vt, p.astype(BF16), NN)


def score_kernel(q_ref, do_ref, begin_ref, kv_ref, s_out, dp_out, m_out, kt_out, vt_out, *, distance):
    heads, rows, hd = q_ref.shape
    scale = LOG2E / math.sqrt(hd)
    kpos = lax.broadcasted_iota(jnp.int32, (rows, 1), 0) - distance * rows
    hide = jnp.where(kpos >= begin_ref[...], 0.0, -jnp.inf)
    k = kv_ref[0:rows, :]
    v = kv_ref[rows:, :]
    for h in range(heads):
        s = dot(k, q_ref[h], NT) * scale + hide
        s_out[h] = s
        m_out[h] = fold(s, jnp.max)
        dp_out[h] = dot(v, do_ref[h], NT).astype(BF16)
    kt_out[...] = k.T
    vt_out[0:hd, :] = v.T
    vt_out[hd:, :] = jnp.ones((vt_out.shape[0] - hd, rows), BF16)


def remote_kernel(q_ref, do_ref, dot_t, m_own, l_own, o_own, *refs):
    parts = [refs[i * REACH : (i + 1) * REACH] for i in range(5)]
    s_in, dp_in, m_in, vt, back = parts
    ds_out, o_out, st_out, q_low, do_low, p_buf = refs[5 * REACH :]
    heads, rows, hd = q_ref.shape
    factor = 1.0 / math.sqrt(hd)
    blocks = [slice(b * rows, (b + 1) * rows) for b in range(REACH)]
    tiles = [(b, slice(c, c + CHUNK)) for b in range(REACH) for c in range(0, rows, CHUNK)]
    def weights(h):
        top = m_in[0][h]
        for b in range(1, REACH):
            top = jnp.maximum(top, m_in[b][h])
        m = jnp.maximum(m_own[h], jnp.max(top, axis=0, keepdims=True))
        st_out[h, 0:1, :] = m
        for b, cs in tiles:
            at = slice(b * rows + cs.start, b * rows + cs.stop)
            p_buf[h, at, :] = jnp.exp2(s_in[b][h, cs, :] - m).astype(BF16)

    def output(h):
        w = jnp.exp2(m_own[h] - st_out[h, 0:1, :])
        o = dot(vt[0][...], p_buf[h, blocks[0], :], NN)
        for b in range(1, REACH):
            o = o + dot(vt[b][...], p_buf[h, blocks[b], :], NN)
        inv = 1.0 / (o[hd : hd + 1, :] + w * l_own[h])
        o = (o[0:hd, :] + w * o_own[h]) * inv
        o_out[h] = o
        st_out[h, 1:2, :] = inv
        st_out[h, 2:3, :] = jnp.sum(fold(o * dot_t[h].astype(F32), jnp.sum), axis=0, keepdims=True)

    def scaled(h):
        col = jnp.broadcast_to(st_out[h, 1:2, :], (8, rows)).T[:, 0:1]
        q_low[h] = (q_ref[h].astype(F32) * col).astype(BF16)
        do_low[h] = (do_ref[h].astype(F32) * col).astype(BF16)

    def slopes(h):
        low = st_out[h, 2:3, :].astype(BF16)
        for b, cs in tiles:
            at = slice(b * rows + cs.start, b * rows + cs.stop)
            ds_out[h, at, :] = p_buf[h, at, :] * (dp_in[b][h, cs, :] - low)

    def each(first, count, *stages):
        @pl.loop(first, first + count)
        def _(h):
            for i, stage in enumerate(stages):
                stage(h - i)

    each(0, heads, weights)
    for h in range(heads):
        output(h)
    for h in range(heads):
        scaled(h); slopes(h)
    dk = dv = None
    for h in range(heads):
        x = dot(ds_out[h], q_low[h], NN)
        y = dot(p_buf[h], do_low[h], NN)
        dk = x if h == 0 else dk + x
        dv = y if h == 0 else dv + y
    for b, bs in enumerate(blocks):
        back[b][0:rows, :] = (dk[bs, :] * factor).astype(BF16)
        back[b][rows:, :] = dv[bs, :].astype(BF16)


def own_kernel(q_low, do_low, s_own, dp_own, st_ref, o_ref, ds_ref, kv_ref, *refs):
    kt = refs[:REACH]
    out_ref, dq_ref, mine_ref = refs[REACH:]
    heads, hd, rows = o_ref.shape
    factor = 1.0 / math.sqrt(hd)
    own_t = kv_ref[0:rows, :].T
    dk = dv = None
    for h in range(heads):
        hs = slice(h * hd, (h + 1) * hd)
        p = jnp.exp2(s_own[h] - st_ref[h, 0:1, :]).astype(BF16)
        ds = p * (dp_own[h] - st_ref[h, 2:3, :].astype(BF16))
        out_ref[:, hs] = o_ref[h].T.astype(BF16)
        g = dot(own_t, ds, NN)
        for b in range(REACH):
            g = g + dot(kt[b][...], ds_ref[h, b * rows : (b + 1) * rows, :], NN)
        dq_ref[:, hs] = (g * (st_ref[h, 1:2, :] * factor)).T.astype(BF16)
        x = dot(ds, q_low[h], NN)
        y = dot(p, do_low[h], NN)
        dk = x if h == 0 else dk + x
        dv = y if h == 0 else dv + y
    mine_ref[0:rows, :] = dk * factor
    mine_ref[rows:, :] = dv


def call(kernel, name, outs, scratch, vmem, flops, *args, in_hbm=0):
    vm = pl.BlockSpec(memory_space=pltpu.VMEM)
    hbm = pl.BlockSpec(memory_space=pltpu.HBM)
    moved = sum(math.prod(a.shape) * a.dtype.itemsize for a in args)
    return pl.pallas_call(
        kernel,
        out_shape=[jax.ShapeDtypeStruct(*o) for o in outs],
        in_specs=[hbm] * in_hbm + [vm] * (len(args) - in_hbm),
        out_specs=[vm] * len(outs),
        scratch_shapes=[pltpu.VMEM(*s) if isinstance(s, tuple) else s for s in scratch],
        compiler_params=pltpu.CompilerParams(vmem_limit_bytes=int(vmem * 2**20)),
        cost_estimate=pl.CostEstimate(flops=flops, bytes_accessed=moved, transcendentals=0),
        name=name,
    )(*(pltpu.with_memory_space_constraint(a, pltpu.HBM) for a in args[:in_hbm]), *args[in_hbm:])


def stage(k, v):
    rows, hd = k.shape
    return call(
        stage_kernel, "stage", [((2 * rows, hd), BF16)], [pltpu.SemaphoreType.DMA((2,))],
        STAGE_MB, 0, k, v, in_hbm=2,
    )[0]


def attention_grads(lens, q, do, packed, far, first_of):
    rows, hd = packed.shape[0] // 2, packed.shape[1]
    heads = q.shape[1] // hd
    width = REACH * rows
    block = 2 * heads * rows * rows * hd
    stack = ((heads, rows, hd), BF16)
    tall = (heads, hd, rows)
    line = ((heads, 1, rows), F32)
    square = (heads, rows, rows)
    qs, dos, dot_t, begin, s_own, dp_own, m_own, l_own, o_own = call(
        functools.partial(local_kernel, first_of=first_of),
        "local",
        [stack, stack, (tall, BF16), ((1, rows), jnp.int32), (square, F32), (square, BF16), line, line, (tall, F32)],
        [((1, lens.shape[0]), jnp.int32), (q.shape, BF16), (do.shape, BF16), pltpu.SemaphoreType.DMA((3,))],
        16, 3 * block, lens.reshape(1, -1), q, do, packed, in_hbm=3,
    )
    scored = [
        call(
            functools.partial(score_kernel, distance=REACH - b),
            "score",
            [(square, F32), (square, BF16), ((heads, 8, rows), F32), ((hd, rows), BF16), ((hd + 8, rows), BF16)],
            [], 12, 2 * block, qs, dos, begin, far[b],
        )
        for b in range(REACH)
    ]
    s, dp, m, kt, vt = zip(*scored)
    *back, ds, o, st, q_low, do_low = call(
        remote_kernel,
        "remote",
        [((2 * rows, hd), BF16)] * REACH
        + [((heads, width, rows), BF16), (tall, F32), ((heads, 3, rows), F32), stack, stack],
        [((heads, width, rows), BF16)],
        16, 12 * block, qs, dos, dot_t, m_own, l_own, o_own, *s, *dp, *m, *vt,
    )
    return back, lambda: call(
        own_kernel,
        "own",
        [(q.shape, BF16)] * 2 + [((2 * rows, hd), F32)],
        [],
        12, 7 * block, q_low, do_low, s_own, dp_own, st, o, ds, packed, *kt,
    )


def shifted(block, distance):
    count = lax.axis_size("ctx") * lax.axis_size("grp")
    route = [(i, (i + distance) % count) for i in range(count)]
    return lax.ppermute(block, ("ctx", "grp"), route)


def body(queries, key_rows, value_rows, out_grad, doc_lengths):
    rows, hd = key_rows.shape

    def first_of():
        return (lax.axis_index("ctx") * lax.axis_size("grp") + lax.axis_index("grp")) * rows

    packed = stage(key_rows, value_rows)
    far = [shifted(packed, d) for d in range(REACH, 0, -1)]
    back, finish = attention_grads(
        doc_lengths, queries, out_grad, packed, far, first_of
    )
    came = [shifted(back[REACH - d], -d) for d in range(REACH, 0, -1)]
    attended, query_grad, total = finish()
    for part in came:
        total = total + part.astype(F32)
    total = total.astype(BF16)
    return attended, query_grad, total[:rows], total[rows:]


def solution(mesh):
    split = P(("ctx", "grp"), None)
    return jax.shard_map(
        body, mesh=mesh, in_specs=(split,) * 4 + (P(),), out_specs=(split,) * 4, check_vma=False
    )
```

time: 41 us -> 39 us (0.951)
  Pallas kernels: 15.4 us -> 13.8 us
  starting transfers between devices: 22.1 us -> 21 us
  waiting for transfers between devices: 1.93 us -> 2.59 us
    pallas_call x4 -> x8, Pallas kernels: 15.4 us -> 13.8 us  [call(): pl.pallas_call(kernel, out_shape=[jax.ShapeDtypeStruct(*o) for o in outs]...]
    ppermute x8, starting transfers between devices: 22.1 us -> 21 us  [shifted(): return lax.ppermute(block, ('ctx', 'grp'), route)]
    ppermute x8, waiting for transfers between devices: 1.93 us -> 2.59 us  [shifted(): return lax.ppermute(block, ('ctx', 'grp'), route)]
  transfers between devices with their start and end apart: 8 -> 8, of which waited for: 2 -> 2; matrix products, arithmetic and copies ran while one was open for 0% -> 0% of each run, Pallas kernels for 15% -> 19%
where the time goes in v4:
time: 39 us; the launch traced here: 38.9 us
  starting transfers between devices  21 us (54%)
  Pallas kernels  13.8 us (35%)
  waiting for transfers between devices  2.59 us (7%)
  between operations  0.73 us (2%)
  local copies, waits for them, and re-layouts  0.66 us (2%)
    ppermute x8, starting transfers between devices, shifted(): return lax.ppermute(block, ('ctx', 'grp'), route)  21 us
    pallas_call x8, Pallas kernels, call(): pl.pallas_call(kernel, out_shape=[jax.ShapeDtypeStruct(*o) for o in outs]...  13.8 us
    ppermute x8, waiting for transfers between devices, shifted(): return lax.ppermute(block, ('ctx', 'grp'), route)  2.59 us
  transfers between devices with their start and end apart: 8, of which 2 were waited for; matrix products, arithmetic and copies ran while one was open for 0% of the time, Pallas kernels for 19%

profile of v4, /device:TPU:1, one launch (start us, length us, event | category | flops | bytes accessed | tf_op | source)
XLA Modules:
  0.0 38.9 jit_solution(8092987983641507661)
XLA Ops:
  0.6 0.9 %stage.1.kv_ref = bf16[512,128]{1,0:T(8,128)(2,1)S(1)} custom-call(bf16[256,128]{1,0:T(8,128)(2,1)} %k_hbm.1, bf16[256,128]{1,0:T(8,128)(2,1)} %v_hbm.1), custom_call_target="tpu_custom_call" | custom-call | bytes 131072 | tf_op jit(solution)/shard_map/stage/pallas_call | solution.py:191
  1.5 2.1 %collective-permute-start.3 = (bf16[512,128]{1,0:T(8,128)(2,1)S(1)}, bf16[512,128]{1,0:T(8,128)(2,1)S(1)}, u32[]{:S(2)}, u32[]{:S(2)}) collective-permute-start(bf16[512,128]{1,0:T(8,128)(2,1)S(1)} %stage.1.kv_ref), channel_id=1, source_target_pairs={{0,1},{1,2},{2,3},{3,4},{4,5},{5,6},{6,7},{7,8},{8,9},{9,10},{10,1... | collective-permute-start | bytes 393224 | tf_op jit(solution)/shard_map/ppermute | solution.py:257
  3.7 2.5 %collective-permute-start.2 = (bf16[512,128]{1,0:T(8,128)(2,1)S(1)}, bf16[512,128]{1,0:T(8,128)(2,1)S(1)}, u32[]{:S(2)}, u32[]{:S(2)}) collective-permute-start(bf16[512,128]{1,0:T(8,128)(2,1)S(1)} %stage.1.kv_ref), channel_id=1, source_target_pairs={{0,2},{1,3},{2,4},{3,5},{4,6},{5,7},{6,8},{7,9},{8,10},{9,11},{10,... | collective-permute-start | bytes 393224 | tf_op jit(solution)/shard_map/ppermute | solution.py:257
  6.1 3.3 %collective-permute-start.1 = (bf16[512,128]{1,0:T(8,128)(2,1)S(1)}, bf16[512,128]{1,0:T(8,128)(2,1)S(1)}, u32[]{:S(2)}, u32[]{:S(2)}) collective-permute-start(bf16[512,128]{1,0:T(8,128)(2,1)S(1)} %stage.1.kv_ref), channel_id=1, source_target_pairs={{0,3},{1,4},{2,5},{3,6},{4,7},{5,8},{6,9},{7,10},{8,11},{9,12},{10... | collective-permute-start | bytes 393224 | tf_op jit(solution)/shard_map/ppermute | solution.py:257
  9.5 0.0 collective-permute-start
  9.5 2.9 %local.1 = (bf16[8,256,128]{2,1,0:T(8,128)(2,1)S(1)}, bf16[8,256,128]{2,1,0:T(8,128)(2,1)S(1)}, bf16[8,128,256]{2,1,0:T(8,128)(2,1)S(1)}, s32[1,256]{1,0:T(1,128...) custom-call(s32[1,128]{1,0:T(1,128)} %bitcast.1, ...), custom_call_target="tpu_custom_call" | custom-call | flops 402653184 | bytes 1180160 | tf_op jit(solution)/shard_map/local/pallas_call | solution.py:191
  12.4 0.0 collective-permute-done.3.kv_ref
  12.4 0.7 %score.7 = (f32[8,256,256]{2,1,0:T(8,128)S(1)}, bf16[8,256,256]{2,1,0:T(8,128)(2,1)S(1)}, f32[8,8,256]{2,1,0:T(8,128)S(1)}, bf16[128,256]{1,0:T(8,128)(2,1)S(1)}, bf16[136,256]{1,0:T(8,128)(2,1)S(1)}) custom-call(bf16[8,256,128]{2,1,0:T(8,128)(2,1)S(1)} %get-tuple-element.45.q_ref, bf16[8,256,128]{2,1,0:T(8,128)(2,1)S(1)} %get-tuple-element.46.do_ref, ...), custom_call_target="tpu_custom_call" | custom-call | flops 268435456 | bytes 1180672 | tf_op jit(solution)/shard_map/score/pallas_call | solution.py:191
  13.1 0.0 collective-permute-done.2.kv_ref
  13.1 0.7 %score.6 = (f32[8,256,256]{2,1,0:T(8,128)S(1)}, bf16[8,256,256]{2,1,0:T(8,128)(2,1)S(1)}, f32[8,8,256]{2,1,0:T(8,128)S(1)}, bf16[128,256]{1,0:T(8,128)(2,1)S(1)}, bf16[136,256]{1,0:T(8,128)(2,1)S(1)}) custom-call(bf16[8,256,128]{2,1,0:T(8,128)(2,1)S(1)} %get-tuple-element.45.q_ref, bf16[8,256,128]{2,1,0:T(8,128)(2,1)S(1)} %get-tuple-element.46.do_ref, ...), custom_call_target="tpu_custom_call" | custom-call | flops 268435456 | bytes 1180672 | tf_op jit(solution)/shard_map/score/pallas_call | solution.py:191
  13.8 0.0 collective-permute-done.1.kv_ref
  13.9 0.7 %score.5 = (f32[8,256,256]{2,1,0:T(8,128)S(1)}, bf16[8,256,256]{2,1,0:T(8,128)(2,1)S(1)}, f32[8,8,256]{2,1,0:T(8,128)S(1)}, bf16[128,256]{1,0:T(8,128)(2,1)S(1)}, bf16[136,256]{1,0:T(8,128)(2,1)S(1)}) custom-call(bf16[8,256,128]{2,1,0:T(8,128)(2,1)S(1)} %get-tuple-element.45.q_ref, bf16[8,256,128]{2,1,0:T(8,128)(2,1)S(1)} %get-tuple-element.46.do_ref, ...), custom_call_target="tpu_custom_call" | custom-call | flops 268435456 | bytes 1180672 | tf_op jit(solution)/shard_map/score/pallas_call | solution.py:191
  14.6 0.0 collective-permute-done.kv_ref
  14.6 0.7 %score.4 = (f32[8,256,256]{2,1,0:T(8,128)S(1)}, bf16[8,256,256]{2,1,0:T(8,128)(2,1)S(1)}, f32[8,8,256]{2,1,0:T(8,128)S(1)}, bf16[128,256]{1,0:T(8,128)(2,1)S(1)}, bf16[136,256]{1,0:T(8,128)(2,1)S(1)}) custom-call(bf16[8,256,128]{2,1,0:T(8,128)(2,1)S(1)} %get-tuple-element.45.q_ref, bf16[8,256,128]{2,1,0:T(8,128)(2,1)S(1)} %get-tuple-element.46.do_ref, ...), custom_call_target="tpu_custom_call" | custom-call | flops 268435456 | bytes 1180672 | tf_op jit(solution)/shard_map/score/pallas_call | solution.py:191
  15.3 4.7 %remote.1 = (bf16[512,128]{1,0:T(8,128)(2,1)S(1)}, bf16[512,128]{1,0:T(8,128)(2,1)S(1)}, bf16[512,128]{1,0:T(8,128)(2,1)S(1)}, bf16[512,128]{1,0:T(8,128)(2,1)S(...) custom-call(bf16[8,256,128]{2,1,0:T(8,128)(2,1)S(1)} %get-tuple-elem, ...), custom_call_target="tpu_custom_call" | custom-call | flops 1610612736 | bytes 15761408 | tf_op jit(solution)/shard_map/remote/pallas_call | solution.py:191
  20.0 6.8 %collective-permute-start.4 = (bf16[512,128]{1,0:T(8,128)(2,1)S(1)}, bf16[512,128]{1,0:T(8,128)(2,1)S(1)}, u32[]{:S(2)}, u32[]{:S(2)}) collective-permute-start(bf16[512,128]{1,0:T(8,128)(2,1)S(1)} %get-tuple-element.82), channel_id=1, source_target_pairs={{0,252},{1,253},{2,254},{3,255},{4,0},{5,1},{6,2},{7,3},{8,4},{9,5... | collective-permute-start | bytes 393224 | tf_op jit(solution)/shard_map/ppermute | solution.py:257
  26.9 2.6 %collective-permute-start.5 = (bf16[512,128]{1,0:T(8,128)(2,1)S(1)}, bf16[512,128]{1,0:T(8,128)(2,1)S(1)}, u32[]{:S(2)}, u32[]{:S(2)}) collective-permute-start(bf16[512,128]{1,0:T(8,128)(2,1)S(1)} %get-tuple-element.83), channel_id=1, source_target_pairs={{0,253},{1,254},{2,255},{3,0},{4,1},{5,2},{6,3},{7,4},{8,5},{9,6},... | collective-permute-start | bytes 393224 | tf_op jit(solution)/shard_map/ppermute | solution.py:257
  29.5 1.3 %collective-permute-start.6 = (bf16[512,128]{1,0:T(8,128)(2,1)S(1)}, bf16[512,128]{1,0:T(8,128)(2,1)S(1)}, u32[]{:S(2)}, u32[]{:S(2)}) collective-permute-start(bf16[512,128]{1,0:T(8,128)(2,1)S(1)} %get-tuple-element.84), channel_id=1, source_target_pairs={{0,254},{1,255},{2,0},{3,1},{4,2},{5,3},{6,4},{7,5},{8,6},{9,7},{1... | collective-permute-start | bytes 393224 | tf_op jit(solution)/shard_map/ppermute | solution.py:257
  30.7 2.3 %collective-permute-start.7 = (bf16[512,128]{1,0:T(8,128)(2,1)S(1)}, bf16[512,128]{1,0:T(8,128)(2,1)S(1)}, u32[]{:S(2)}, u32[]{:S(2)}) collective-permute-start(bf16[512,128]{1,0:T(8,128)(2,1)S(1)} %get-tuple-element.85), channel_id=1, source_target_pairs={{0,255},{1,0},{2,1},{3,2},{4,3},{5,4},{6,5},{7,6},{8,7},{9,8},{10,... | collective-permute-start | bytes 393224 | tf_op jit(solution)/shard_map/ppermute | solution.py:257
  33.1 2.5 %own.1 = (bf16[256,1024]{1,0:T(8,128)(2,1)}, bf16[256,1024]{1,0:T(8,128)(2,1)}, f32[512,128]{1,0:T(8,128)S(1)}) custom-call(bf16[8,256,128]{2,1,0:T(8,128)(2,1)S(1)} %get-tuple-element.68.q_low, bf16[8,256,128]{2,1,0:T(8,128)(2,1)S(1)} %get-tuple-element.69.do_low, f32[8,256,256]{2,1,0:T(8,128)S(1)} %get-tuple-element.70.s_own, ...), custom_call_target="tpu_custom_call" | custom-call | flops 939524096 | bytes 9854976 | tf_op jit(solution)/shard_map/own/pallas_call | solution.py:191
  35.6 0.0 collective-permute-done.4
  35.6 0.0 collective-permute-done.5
  35.6 0.5 %collective-permute-done.6 = bf16[512,128]{1,0:T(8,128)(2,1)S(1)} collective-permute-done((bf16[512,128]{1,0:T(8,128)(2,1)S(1)}, bf16[512,128]{1,0:T(8,128)(2,1)S(1)}, u32[]{:S(2)}, u32[]{:S(2)}) %collective-permute-start.6) | collective-permute-done | bytes 131104 | tf_op jit(solution)/shard_map/ppermute | solution.py:257
  36.1 2.1 %collective-permute-done.7 = bf16[512,128]{1,0:T(8,128)(2,1)S(1)} collective-permute-done((bf16[512,128]{1,0:T(8,128)(2,1)S(1)}, bf16[512,128]{1,0:T(8,128)(2,1)S(1)}, u32[]{:S(2)}, u32[]{:S(2)}) %collective-permute-start.7) | collective-permute-done | bytes 131104 | tf_op jit(solution)/shard_map/ppermute | solution.py:257
  38.1 0.1 add_convert_fusion
  38.2 0.7 %fusion = (bf16[256,128]{1,0:T(8,128)(2,1)}, bf16[256,128]{1,0:T(8,128)(2,1)}) fusion(bf16[512,128]{1,0:T(8,128)(2,1)S(1)} %add_convert_fusion), kind=kLoop, calls=%fused_computation.1 | loop fusion | bytes 262144 | tf_op jit(solution)/shard_map/slice | solution.py:276
Async XLA Ops:
  1.5 10.8 %collective-permute-start.3 = (bf16[512,128]{1,0:T(8,128)(2,1)S(1)}, bf16[512,128]{1,0:T(8,128)(2,1)S(1)}, u32[]{:S(2)}, u32[]{:S(2)}) collective-permute-start(bf16[512,128]{1,0:T(8,128)(2,1)S(1)} %stage.1.kv_ref), channel_id=1, source_target_pairs={{0,1},{1,2},{2,3},{3,4},{4,5},{5,6},{6,7},{7,8},{8,9},{9,10},{10,1... | collective-permute-start | bytes 393224 | tf_op jit(solution)/shard_map/ppermute | solution.py:257
  3.7 9.5 %collective-permute-start.2 = (bf16[512,128]{1,0:T(8,128)(2,1)S(1)}, bf16[512,128]{1,0:T(8,128)(2,1)S(1)}, u32[]{:S(2)}, u32[]{:S(2)}) collective-permute-start(bf16[512,128]{1,0:T(8,128)(2,1)S(1)} %stage.1.kv_ref), channel_id=1, source_target_pairs={{0,2},{1,3},{2,4},{3,5},{4,6},{5,7},{6,8},{7,9},{8,10},{9,11},{10,... | collective-permute-start | bytes 393224 | tf_op jit(solution)/shard_map/ppermute | solution.py:257
  6.1 7.7 %collective-permute-start.1 = (bf16[512,128]{1,0:T(8,128)(2,1)S(1)}, bf16[512,128]{1,0:T(8,128)(2,1)S(1)}, u32[]{:S(2)}, u32[]{:S(2)}) collective-permute-start(bf16[512,128]{1,0:T(8,128)(2,1)S(1)} %stage.1.kv_ref), channel_id=1, source_target_pairs={{0,3},{1,4},{2,5},{3,6},{4,7},{5,8},{6,9},{7,10},{8,11},{9,12},{10... | collective-permute-start | bytes 393224 | tf_op jit(solution)/shard_map/ppermute | solution.py:257
  9.5 5.1 %collective-permute-start = (bf16[512,128]{1,0:T(8,128)(2,1)S(1)}, bf16[512,128]{1,0:T(8,128)(2,1)S(1)}, u32[]{:S(2)}, u32[]{:S(2)}) collective-permute-start(bf16[512,128]{1,0:T(8,128)(2,1)S(1)} %stage.1.kv_ref), channel_id=1, source_target_pairs={{0,4},{1,5},{2,6},{3,7},{4,8},{5,9},{6,10},{7,11},{8,12},{9,13},{1... | collective-permute-start | bytes 393224 | tf_op jit(solution)/shard_map/ppermute | solution.py:257
  20.0 15.6 %collective-permute-start.4 = (bf16[512,128]{1,0:T(8,128)(2,1)S(1)}, bf16[512,128]{1,0:T(8,128)(2,1)S(1)}, u32[]{:S(2)}, u32[]{:S(2)}) collective-permute-start(bf16[512,128]{1,0:T(8,128)(2,1)S(1)} %get-tuple-element.82), channel_id=1, source_target_pairs={{0,252},{1,253},{2,254},{3,255},{4,0},{5,1},{6,2},{7,3},{8,4},{9,5... | collective-permute-start | bytes 393224 | tf_op jit(solution)/shard_map/ppermute | solution.py:257
  26.9 8.7 %collective-permute-start.5 = (bf16[512,128]{1,0:T(8,128)(2,1)S(1)}, bf16[512,128]{1,0:T(8,128)(2,1)S(1)}, u32[]{:S(2)}, u32[]{:S(2)}) collective-permute-start(bf16[512,128]{1,0:T(8,128)(2,1)S(1)} %get-tuple-element.83), channel_id=1, source_target_pairs={{0,253},{1,254},{2,255},{3,0},{4,1},{5,2},{6,3},{7,4},{8,5},{9,6},... | collective-permute-start | bytes 393224 | tf_op jit(solution)/shard_map/ppermute | solution.py:257
  29.5 6.6 %collective-permute-start.6 = (bf16[512,128]{1,0:T(8,128)(2,1)S(1)}, bf16[512,128]{1,0:T(8,128)(2,1)S(1)}, u32[]{:S(2)}, u32[]{:S(2)}) collective-permute-start(bf16[512,128]{1,0:T(8,128)(2,1)S(1)} %get-tuple-element.84), channel_id=1, source_target_pairs={{0,254},{1,255},{2,0},{3,1},{4,2},{5,3},{6,4},{7,5},{8,6},{9,7},{1... | collective-permute-start | bytes 393224 | tf_op jit(solution)/shard_map/ppermute | solution.py:257
  30.7 7.4 %collective-permute-start.7 = (bf16[512,128]{1,0:T(8,128)(2,1)S(1)}, bf16[512,128]{1,0:T(8,128)(2,1)S(1)}, u32[]{:S(2)}, u32[]{:S(2)}) collective-permute-start(bf16[512,128]{1,0:T(8,128)(2,1)S(1)} %get-tuple-element.85), channel_id=1, source_target_pairs={{0,255},{1,0},{2,1},{3,2},{4,3},{5,4},{6,5},{7,6},{8,7},{9,8},{10,... | collective-permute-start | bytes 393224 | tf_op jit(solution)/shard_map/ppermute | solution.py:257

commit v5 on v4

--- a/solution.py
+++ b/solution.py
@@ -75,7 +75,7 @@
         m = jnp.max(fold(s, jnp.max), axis=0, keepdims=True)
         p = jnp.exp2(s - m)
         s_own[h] = s
-        dp_own[h] = dot(kv_ref[rows:, :], do, NT).astype(BF16)
+        dp_own[h] = dot(kv_ref[rows:, :], do, NT)
         m_own[h] = m
         l_own[h] = jnp.sum(fold(p, jnp.sum), axis=0, keepdims=True)
         o_own[h] = dot(vt, p.astype(BF16), NN)
@@ -88,29 +88,31 @@
     hide = jnp.where(kpos >= begin_ref[...], 0.0, -jnp.inf)
     k = kv_ref[0:rows, :]
     v = kv_ref[rows:, :]
-    for h in range(heads):
-        s = dot(k, q_ref[h], NT) * scale + hide
-        s_out[h] = s
-        m_out[h] = fold(s, jnp.max)
-        dp_out[h] = dot(v, do_ref[h], NT).astype(BF16)
     kt_out[...] = k.T
     vt_out[0:hd, :] = v.T
     vt_out[hd:, :] = jnp.ones((vt_out.shape[0] - hd, rows), BF16)
 
-
-def remote_kernel(q_ref, do_ref, dot_t, m_own, l_own, o_own, *refs):
+    @pl.when(jnp.min(begin_ref[...]) < (1 - distance) * rows)
+    def _():
+        for h in range(heads):
+            s = dot(k, q_ref[h], NT) * scale + hide
+            s_out[h] = s
+            m_out[h] = fold(s, jnp.max)
+            dp_out[h] = dot(v, do_ref[h], NT)
+
+
+def far_blocks(count, q_ref, do_ref, dot_t, m_own, l_own, o_own, *refs):
     parts = [refs[i * REACH : (i + 1) * REACH] for i in range(5)]
     s_in, dp_in, m_in, vt, back = parts
     ds_out, o_out, st_out, q_low, do_low, p_buf = refs[5 * REACH :]
     heads, rows, hd = q_ref.shape
     factor = 1.0 / math.sqrt(hd)
-    blocks = [slice(b * rows, (b + 1) * rows) for b in range(REACH)]
-    tiles = [(b, slice(c, c + CHUNK)) for b in range(REACH) for c in range(0, rows, CHUNK)]
+    seen = range(REACH - count, REACH)
+    tiles = [(b, slice(c, c + CHUNK)) for b in seen for c in range(0, rows, CHUNK)]
     def weights(h):
-        top = m_in[0][h]
-        for b in range(1, REACH):
-            top = jnp.maximum(top, m_in[b][h])
-        m = jnp.maximum(m_own[h], jnp.max(top, axis=0, keepdims=True))
+        m = m_own[h]
+        for b in seen:
+            m = jnp.maximum(m, jnp.max(m_in[b][h], axis=0, keepdims=True))
         st_out[h, 0:1, :] = m
         for b, cs in tiles:
             at = slice(b * rows + cs.start, b * rows + cs.stop)
@@ -118,11 +120,14 @@
 
     def output(h):
         w = jnp.exp2(m_own[h] - st_out[h, 0:1, :])
-        o = dot(vt[0][...], p_buf[h, blocks[0], :], NN)
-        for b in range(1, REACH):
-            o = o + dot(vt[b][...], p_buf[h, blocks[b], :], NN)
-        inv = 1.0 / (o[hd : hd + 1, :] + w * l_own[h])
-        o = (o[0:hd, :] + w * o_own[h]) * inv
+        total = w * l_own[h]
+        o = w * o_own[h]
+        if count:
+            far_o = sum(dot(vt[b][...], p_buf[h, b * rows : (b + 1) * rows, :], NN) for b in seen)
+            total = total + far_o[hd : hd + 1, :]
+            o = o + far_o[0:hd, :]
+        inv = 1.0 / total
+        o = o * inv
         o_out[h] = o
         st_out[h, 1:2, :] = inv
         st_out[h, 2:3, :] = jnp.sum(fold(o * dot_t[h].astype(F32), jnp.sum), axis=0, keepdims=True)
@@ -133,31 +138,46 @@
         do_low[h] = (do_ref[h].astype(F32) * col).astype(BF16)
 
     def slopes(h):
-        low = st_out[h, 2:3, :].astype(BF16)
+        delta = st_out[h, 2:3, :]
         for b, cs in tiles:
             at = slice(b * rows + cs.start, b * rows + cs.stop)
-            ds_out[h, at, :] = p_buf[h, at, :] * (dp_in[b][h, cs, :] - low)
-
-    def each(first, count, *stages):
-        @pl.loop(first, first + count)
-        def _(h):
-            for i, stage in enumerate(stages):
-                stage(h - i)
-
-    each(0, heads, weights)
+            ds_out[h, at, :] = p_buf[h, at, :] * (dp_in[b][h, cs, :] - delta).astype(BF16)
+
+    for h in range(heads):
+        weights(h)
     for h in range(heads):
         output(h)
     for h in range(heads):
         scaled(h); slopes(h)
+    low = (REACH - count) * rows
+    if low:
+        ds_out[:, 0:low, :] = jnp.zeros((heads, low, rows), BF16)
+    for b in range(REACH - count):
+        back[b][...] = jnp.zeros(back[b].shape, BF16)
+    if not count:
+        return
     dk = dv = None
     for h in range(heads):
-        x = dot(ds_out[h], q_low[h], NN)
-        y = dot(p_buf[h], do_low[h], NN)
+        x = dot(ds_out[h, low:, :], q_low[h], NN)
+        y = dot(p_buf[h, low:, :], do_low[h], NN)
         dk = x if h == 0 else dk + x
         dv = y if h == 0 else dv + y
-    for b, bs in enumerate(blocks):
+    for i, b in enumerate(seen):
+        bs = slice(i * rows, (i + 1) * rows)
         back[b][0:rows, :] = (dk[bs, :] * factor).astype(BF16)
         back[b][rows:, :] = dv[bs, :].astype(BF16)
+
+
+def remote_kernel(begin_ref, *refs):
+    first = jnp.min(begin_ref[...])
+    rows = begin_ref.shape[1]
+    for count in range(REACH + 1):
+        near = first < (1 - count) * rows if count else first >= 0
+        far = first >= -count * rows if count < REACH else first < (1 - REACH) * rows
+
+        @pl.when(near & far)
+        def _(count=count):
+            far_blocks(count, *refs)
 
 
 def own_kernel(q_low, do_low, s_own, dp_own, st_ref, o_ref, ds_ref, kv_ref, *refs):
@@ -170,7 +190,7 @@
     for h in range(heads):
         hs = slice(h * hd, (h + 1) * hd)
         p = jnp.exp2(s_own[h] - st_ref[h, 0:1, :]).astype(BF16)
-        ds = p * (dp_own[h] - st_ref[h, 2:3, :].astype(BF16))
+        ds = p * (dp_own[h] - st_ref[h, 2:3, :]).astype(BF16)
         out_ref[:, hs] = o_ref[h].T.astype(BF16)
         g = dot(own_t, ds, NN)
         for b in range(REACH):
@@ -220,7 +240,7 @@
     qs, dos, dot_t, begin, s_own, dp_own, m_own, l_own, o_own = call(
         functools.partial(local_kernel, first_of=first_of),
         "local",
-        [stack, stack, (tall, BF16), ((1, rows), jnp.int32), (square, F32), (square, BF16), line, line, (tall, F32)],
+        [stack, stack, (tall, BF16), ((1, rows), jnp.int32), (square, F32), (square, F32), line, line, (tall, F32)],
         [((1, lens.shape[0]), jnp.int32), (q.shape, BF16), (do.shape, BF16), pltpu.SemaphoreType.DMA((3,))],
         16, 3 * block, lens.reshape(1, -1), q, do, packed, in_hbm=3,
     )
@@ -228,7 +248,7 @@
         call(
             functools.partial(score_kernel, distance=REACH - b),
             "score",
-            [(square, F32), (square, BF16), ((heads, 8, rows), F32), ((hd, rows), BF16), ((hd + 8, rows), BF16)],
+            [(square, F32), (square, F32), ((heads, 8, rows), F32), ((hd, rows), BF16), ((hd + 8, rows), BF16)],
             [], 12, 2 * block, qs, dos, begin, far[b],
         )
         for b in range(REACH)
@@ -240,7 +260,7 @@
         [((2 * rows, hd), BF16)] * REACH
         + [((heads, width, rows), BF16), (tall, F32), ((heads, 3, rows), F32), stack, stack],
         [((heads, width, rows), BF16)],
-        16, 12 * block, qs, dos, dot_t, m_own, l_own, o_own, *s, *dp, *m, *vt,
+        16, 12 * block, begin, qs, dos, dot_t, m_own, l_own, o_own, *s, *dp, *m, *vt,
     )
     return back, lambda: call(
         own_kernel,

time: 39 us -> 36.8 us (0.944); the launches traced: 38.9 us -> 36.1 us
  Pallas kernels: 13.8 us -> 10.3 us
  starting transfers between devices: 21 us -> 24 us
  waiting for transfers between devices: 2.59 us -> 0.24 us
    pallas_call x8, Pallas kernels: 13.8 us -> 10.3 us  [call(): pl.pallas_call(kernel, out_shape=[jax.ShapeDtypeStruct(*o) for o in outs]...]
    ppermute x8, starting transfers between devices: 21 us -> 24 us  [shifted(): return lax.ppermute(block, ('ctx', 'grp'), route)]
    ppermute x8, waiting for transfers between devices: 2.59 us -> 0.24 us  [shifted(): return lax.ppermute(block, ('ctx', 'grp'), route)]
  transfers between devices with their start and end apart: 8 -> 8, of which waited for: 2 -> 1; matrix products, arithmetic and copies ran while one was open for 0% -> 0% of each run, Pallas kernels for 19% -> 19%
where the time goes in v5:
time: 36.8 us; the launch traced here: 36.1 us
  starting transfers between devices  24 us (65%)
  Pallas kernels  10.3 us (28%)
  between operations  0.73 us (2%)
  local copies, waits for them, and re-layouts  0.66 us (2%)
    ppermute x8, starting transfers between devices, shifted(): return lax.ppermute(block, ('ctx', 'grp'), route)  24 us
    pallas_call x8, Pallas kernels, call(): pl.pallas_call(kernel, out_shape=[jax.ShapeDtypeStruct(*o) for o in outs]...  10.3 us
  transfers between devices with their start and end apart: 8, of which 1 were waited for; matrix products, arithmetic and copies ran while one was open for 0% of the time, Pallas kernels for 19%

profile of v5, /device:TPU:1, one launch (start us, length us, event | category | flops | bytes accessed | tf_op | source)
XLA Modules:
  0.0 36.1 jit_solution(16680490767133197903)
XLA Ops:
  0.6 0.9 %stage.1.kv_ref = bf16[512,128]{1,0:T(8,128)(2,1)S(1)} custom-call(bf16[256,128]{1,0:T(8,128)(2,1)} %k_hbm.1, bf16[256,128]{1,0:T(8,128)(2,1)} %v_hbm.1), custom_call_target="tpu_custom_call" | custom-call | bytes 131072 | tf_op jit(solution)/shard_map/stage/pallas_call | solution.py:211
  1.5 2.1 %collective-permute-start.3 = (bf16[512,128]{1,0:T(8,128)(2,1)S(1)}, bf16[512,128]{1,0:T(8,128)(2,1)S(1)}, u32[]{:S(2)}, u32[]{:S(2)}) collective-permute-start(bf16[512,128]{1,0:T(8,128)(2,1)S(1)} %stage.1.kv_ref), channel_id=1, source_target_pairs={{0,1},{1,2},{2,3},{3,4},{4,5},{5,6},{6,7},{7,8},{8,9},{9,10},{10,1... | collective-permute-start | bytes 393224 | tf_op jit(solution)/shard_map/ppermute | solution.py:277
  3.7 2.5 %collective-permute-start.2 = (bf16[512,128]{1,0:T(8,128)(2,1)S(1)}, bf16[512,128]{1,0:T(8,128)(2,1)S(1)}, u32[]{:S(2)}, u32[]{:S(2)}) collective-permute-start(bf16[512,128]{1,0:T(8,128)(2,1)S(1)} %stage.1.kv_ref), channel_id=1, source_target_pairs={{0,2},{1,3},{2,4},{3,5},{4,6},{5,7},{6,8},{7,9},{8,10},{9,11},{10,... | collective-permute-start | bytes 393224 | tf_op jit(solution)/shard_map/ppermute | solution.py:277
  6.1 3.3 %collective-permute-start.1 = (bf16[512,128]{1,0:T(8,128)(2,1)S(1)}, bf16[512,128]{1,0:T(8,128)(2,1)S(1)}, u32[]{:S(2)}, u32[]{:S(2)}) collective-permute-start(bf16[512,128]{1,0:T(8,128)(2,1)S(1)} %stage.1.kv_ref), channel_id=1, source_target_pairs={{0,3},{1,4},{2,5},{3,6},{4,7},{5,8},{6,9},{7,10},{8,11},{9,12},{10... | collective-permute-start | bytes 393224 | tf_op jit(solution)/shard_map/ppermute | solution.py:277
  9.5 0.0 collective-permute-start
  9.5 2.9 %local.1 = (bf16[8,256,128]{2,1,0:T(8,128)(2,1)S(1)}, bf16[8,256,128]{2,1,0:T(8,128)(2,1)S(1)}, bf16[8,128,256]{2,1,0:T(8,128)(2,1)S(1)}, s32[1,256]{1,0:T(1,128...) custom-call(s32[1,128]{1,0:T(1,128)} %bitcast.1, ...), custom_call_target="tpu_custom_call" | custom-call | flops 402653184 | bytes 1180160 | tf_op jit(solution)/shard_map/local/pallas_call | solution.py:211
  12.4 0.0 collective-permute-done.3.kv_ref
  12.4 0.9 %score.7 = (f32[8,256,256]{2,1,0:T(8,128)S(1)}, f32[8,256,256]{2,1,0:T(8,128)S(1)}, f32[8,8,256]{2,1,0:T(8,128)S(1)}, bf16[128,256]{1,0:T(8,128)(2,1)S(1)}, bf16[136,256]{1,0:T(8,128)(2,1)S(1)}) custom-call(bf16[8,256,128]{2,1,0:T(8,128)(2,1)S(1)} %get-tuple-element.46.q_ref.refs_0_, bf16[8,256,128]{2,1,0:T(8,128)(2,1)S(1)} %get-tuple-element.47.do_ref.refs_1_, ...), custom_call_target="tpu_custom_call" | custom-call | flops 268435456 | bytes 1180672 | tf_op jit(solution)/shard_map/score/pallas_call | solution.py:211
  13.3 0.0 collective-permute-done.2.kv_ref
  13.3 0.2 score.6
  13.5 0.0 collective-permute-done.1.kv_ref
  13.6 0.2 score.5
  13.8 0.0 collective-permute-done.kv_ref
  13.8 0.2 score.4
  14.0 2.4 %remote.1 = (bf16[512,128]{1,0:T(8,128)(2,1)S(1)}, bf16[512,128]{1,0:T(8,128)(2,1)S(1)}, bf16[512,128]{1,0:T(8,128)(2,1)S(1)}, bf16[512,128]{1,0:T(8,128)(2,1)S(...) custom-call(s32[1,256]{1,0:T(1,128)S(1)} %get-tuple-element.45.begin, ...), custom_call_target="tpu_custom_call" | custom-call | flops 1610612736 | bytes 19956736 | tf_op jit(solution)/shard_map/remote/pallas_call | solution.py:211
  16.4 5.8 %collective-permute-start.4 = (bf16[512,128]{1,0:T(8,128)(2,1)S(1)}, bf16[512,128]{1,0:T(8,128)(2,1)S(1)}, u32[]{:S(2)}, u32[]{:S(2)}) collective-permute-start(bf16[512,128]{1,0:T(8,128)(2,1)S(1)} %get-tuple-element.82), channel_id=1, source_target_pairs={{0,252},{1,253},{2,254},{3,255},{4,0},{5,1},{6,2},{7,3},{8,4},{9,5... | collective-permute-start | bytes 393224 | tf_op jit(solution)/shard_map/ppermute | solution.py:277
  22.1 6.5 %collective-permute-start.5 = (bf16[512,128]{1,0:T(8,128)(2,1)S(1)}, bf16[512,128]{1,0:T(8,128)(2,1)S(1)}, u32[]{:S(2)}, u32[]{:S(2)}) collective-permute-start(bf16[512,128]{1,0:T(8,128)(2,1)S(1)} %get-tuple-element.83), channel_id=1, source_target_pairs={{0,253},{1,254},{2,255},{3,0},{4,1},{5,2},{6,3},{7,4},{8,5},{9,6},... | collective-permute-start | bytes 393224 | tf_op jit(solution)/shard_map/ppermute | solution.py:277
  28.6 0.0 collective-permute-start.6
  28.6 3.9 %collective-permute-start.7 = (bf16[512,128]{1,0:T(8,128)(2,1)S(1)}, bf16[512,128]{1,0:T(8,128)(2,1)S(1)}, u32[]{:S(2)}, u32[]{:S(2)}) collective-permute-start(bf16[512,128]{1,0:T(8,128)(2,1)S(1)} %get-tuple-element.85), channel_id=1, source_target_pairs={{0,255},{1,0},{2,1},{3,2},{4,3},{5,4},{6,5},{7,6},{8,7},{9,8},{10,... | collective-permute-start | bytes 393224 | tf_op jit(solution)/shard_map/ppermute | solution.py:277
  32.5 2.6 %own.1 = (bf16[256,1024]{1,0:T(8,128)(2,1)}, bf16[256,1024]{1,0:T(8,128)(2,1)}, f32[512,128]{1,0:T(8,128)S(1)}) custom-call(bf16[8,256,128]{2,1,0:T(8,128)(2,1)S(1)} %get-tuple-element.68.q_low, bf16[8,256,128]{2,1,0:T(8,128)(2,1)S(1)} %get-tuple-element.69.do_low, f32[8,256,256]{2,1,0:T(8,128)S(1)} %get-tuple-element.70.s_own, ...), custom_call_target="tpu_custom_call" | custom-call | flops 939524096 | bytes 10903552 | tf_op jit(solution)/shard_map/own/pallas_call | solution.py:211
  35.1 0.0 collective-permute-done.4
  35.1 0.0 collective-permute-done.5
  35.1 0.2 collective-permute-done.6
  35.3 0.0 collective-permute-done.7
  35.3 0.1 add_convert_fusion
  35.4 0.7 %fusion = (bf16[256,128]{1,0:T(8,128)(2,1)}, bf16[256,128]{1,0:T(8,128)(2,1)}) fusion(bf16[512,128]{1,0:T(8,128)(2,1)S(1)} %add_convert_fusion), kind=kLoop, calls=%fused_computation.1 | loop fusion | bytes 262144 | tf_op jit(solution)/shard_map/slice | solution.py:296
Async XLA Ops:
  1.5 10.8 %collective-permute-start.3 = (bf16[512,128]{1,0:T(8,128)(2,1)S(1)}, bf16[512,128]{1,0:T(8,128)(2,1)S(1)}, u32[]{:S(2)}, u32[]{:S(2)}) collective-permute-start(bf16[512,128]{1,0:T(8,128)(2,1)S(1)} %stage.1.kv_ref), channel_id=1, source_target_pairs={{0,1},{1,2},{2,3},{3,4},{4,5},{5,6},{6,7},{7,8},{8,9},{9,10},{10,1... | collective-permute-start | bytes 393224 | tf_op jit(solution)/shard_map/ppermute | solution.py:277
  3.7 9.7 %collective-permute-start.2 = (bf16[512,128]{1,0:T(8,128)(2,1)S(1)}, bf16[512,128]{1,0:T(8,128)(2,1)S(1)}, u32[]{:S(2)}, u32[]{:S(2)}) collective-permute-start(bf16[512,128]{1,0:T(8,128)(2,1)S(1)} %stage.1.kv_ref), channel_id=1, source_target_pairs={{0,2},{1,3},{2,4},{3,5},{4,6},{5,7},{6,8},{7,9},{8,10},{9,11},{10,... | collective-permute-start | bytes 393224 | tf_op jit(solution)/shard_map/ppermute | solution.py:277
  6.1 7.4 %collective-permute-start.1 = (bf16[512,128]{1,0:T(8,128)(2,1)S(1)}, bf16[512,128]{1,0:T(8,128)(2,1)S(1)}, u32[]{:S(2)}, u32[]{:S(2)}) collective-permute-start(bf16[512,128]{1,0:T(8,128)(2,1)S(1)} %stage.1.kv_ref), channel_id=1, source_target_pairs={{0,3},{1,4},{2,5},{3,6},{4,7},{5,8},{6,9},{7,10},{8,11},{9,12},{10... | collective-permute-start | bytes 393224 | tf_op jit(solution)/shard_map/ppermute | solution.py:277
  9.5 4.3 %collective-permute-start = (bf16[512,128]{1,0:T(8,128)(2,1)S(1)}, bf16[512,128]{1,0:T(8,128)(2,1)S(1)}, u32[]{:S(2)}, u32[]{:S(2)}) collective-permute-start(bf16[512,128]{1,0:T(8,128)(2,1)S(1)} %stage.1.kv_ref), channel_id=1, source_target_pairs={{0,4},{1,5},{2,6},{3,7},{4,8},{5,9},{6,10},{7,11},{8,12},{9,13},{1... | collective-permute-start | bytes 393224 | tf_op jit(solution)/shard_map/ppermute | solution.py:277
  16.4 18.7 %collective-permute-start.4 = (bf16[512,128]{1,0:T(8,128)(2,1)S(1)}, bf16[512,128]{1,0:T(8,128)(2,1)S(1)}, u32[]{:S(2)}, u32[]{:S(2)}) collective-permute-start(bf16[512,128]{1,0:T(8,128)(2,1)S(1)} %get-tuple-element.82), channel_id=1, source_target_pairs={{0,252},{1,253},{2,254},{3,255},{4,0},{5,1},{6,2},{7,3},{8,4},{9,5... | collective-permute-start | bytes 393224 | tf_op jit(solution)/shard_map/ppermute | solution.py:277
  22.1 13.0 %collective-permute-start.5 = (bf16[512,128]{1,0:T(8,128)(2,1)S(1)}, bf16[512,128]{1,0:T(8,128)(2,1)S(1)}, u32[]{:S(2)}, u32[]{:S(2)}) collective-permute-start(bf16[512,128]{1,0:T(8,128)(2,1)S(1)} %get-tuple-element.83), channel_id=1, source_target_pairs={{0,253},{1,254},{2,255},{3,0},{4,1},{5,2},{6,3},{7,4},{8,5},{9,6},... | collective-permute-start | bytes 393224 | tf_op jit(solution)/shard_map/ppermute | solution.py:277
  28.6 6.7 %collective-permute-start.6 = (bf16[512,128]{1,0:T(8,128)(2,1)S(1)}, bf16[512,128]{1,0:T(8,128)(2,1)S(1)}, u32[]{:S(2)}, u32[]{:S(2)}) collective-permute-start(bf16[512,128]{1,0:T(8,128)(2,1)S(1)} %get-tuple-element.84), channel_id=1, source_target_pairs={{0,254},{1,255},{2,0},{3,1},{4,2},{5,3},{6,4},{7,5},{8,6},{9,7},{1... | collective-permute-start | bytes 393224 | tf_op jit(solution)/shard_map/ppermute | solution.py:277
  28.6 6.7 %collective-permute-start.7 = (bf16[512,128]{1,0:T(8,128)(2,1)S(1)}, bf16[512,128]{1,0:T(8,128)(2,1)S(1)}, u32[]{:S(2)}, u32[]{:S(2)}) collective-permute-start(bf16[512,128]{1,0:T(8,128)(2,1)S(1)} %get-tuple-element.85), channel_id=1, source_target_pairs={{0,255},{1,0},{2,1},{3,2},{4,3},{5,4},{6,5},{7,6},{8,7},{9,8},{10,... | collective-permute-start | bytes 393224 | tf_op jit(solution)/shard_map/ppermute | solution.py:277

commit v6 on v5

--- a/solution.py
+++ b/solution.py
@@ -288,7 +288,7 @@
     back, finish = attention_grads(
         doc_lengths, queries, out_grad, packed, far, first_of
     )
-    came = [shifted(back[REACH - d], -d) for d in range(REACH, 0, -1)]
+    came = [shifted(back[REACH - d], -d) for d in range(1, REACH + 1)]
     attended, query_grad, total = finish()
     for part in came:
         total = total + part.astype(F32)

time: 36.8 us -> 34.5 us (0.938)
  starting transfers between devices: 24 us -> 20.2 us
  waiting for transfers between devices: 0.24 us -> 2.08 us
    ppermute x8, starting transfers between devices: 24 us -> 20.2 us  [shifted(): return lax.ppermute(block, ('ctx', 'grp'), route)]
    ppermute x8, waiting for transfers between devices: 0.24 us -> 2.08 us  [shifted(): return lax.ppermute(block, ('ctx', 'grp'), route)]
  transfers between devices with their start and end apart: 8 -> 8, of which waited for: 1 -> 1; matrix products, arithmetic and copies ran while one was open for 0% -> 0% of each run, Pallas kernels for 19% -> 20%
where the time goes in v6:
time: 34.5 us; the launch traced here: 34.1 us
  starting transfers between devices  20.2 us (59%)
  Pallas kernels  10.3 us (30%)
  waiting for transfers between devices  2.08 us (6%)
  between operations  0.73 us (2%)
  local copies, waits for them, and re-layouts  0.66 us (2%)
    ppermute x8, starting transfers between devices, shifted(): return lax.ppermute(block, ('ctx', 'grp'), route)  20.2 us
    pallas_call x8, Pallas kernels, call(): pl.pallas_call(kernel, out_shape=[jax.ShapeDtypeStruct(*o) for o in outs]...  10.3 us
    ppermute x8, waiting for transfers between devices, shifted(): return lax.ppermute(block, ('ctx', 'grp'), route)  2.08 us
  transfers between devices with their start and end apart: 8, of which 1 were waited for; matrix products, arithmetic and copies ran while one was open for 0% of the time, Pallas kernels for 20%

profile of v6, /device:TPU:1, one launch (start us, length us, event | category | flops | bytes accessed | tf_op | source)
XLA Modules:
  0.0 34.1 jit_solution(10837689373750151812)
XLA Ops:
  0.6 0.9 %stage.1.kv_ref = bf16[512,128]{1,0:T(8,128)(2,1)S(1)} custom-call(bf16[256,128]{1,0:T(8,128)(2,1)} %k_hbm.1, bf16[256,128]{1,0:T(8,128)(2,1)} %v_hbm.1), custom_call_target="tpu_custom_call" | custom-call | bytes 131072 | tf_op jit(solution)/shard_map/stage/pallas_call | solution.py:211
  1.5 2.1 %collective-permute-start.3 = (bf16[512,128]{1,0:T(8,128)(2,1)S(1)}, bf16[512,128]{1,0:T(8,128)(2,1)S(1)}, u32[]{:S(2)}, u32[]{:S(2)}) collective-permute-start(bf16[512,128]{1,0:T(8,128)(2,1)S(1)} %stage.1.kv_ref), channel_id=1, source_target_pairs={{0,1},{1,2},{2,3},{3,4},{4,5},{5,6},{6,7},{7,8},{8,9},{9,10},{10,1... | collective-permute-start | bytes 393224 | tf_op jit(solution)/shard_map/ppermute | solution.py:277
  3.7 2.5 %collective-permute-start.2 = (bf16[512,128]{1,0:T(8,128)(2,1)S(1)}, bf16[512,128]{1,0:T(8,128)(2,1)S(1)}, u32[]{:S(2)}, u32[]{:S(2)}) collective-permute-start(bf16[512,128]{1,0:T(8,128)(2,1)S(1)} %stage.1.kv_ref), channel_id=1, source_target_pairs={{0,2},{1,3},{2,4},{3,5},{4,6},{5,7},{6,8},{7,9},{8,10},{9,11},{10,... | collective-permute-start | bytes 393224 | tf_op jit(solution)/shard_map/ppermute | solution.py:277
  6.1 3.3 %collective-permute-start.1 = (bf16[512,128]{1,0:T(8,128)(2,1)S(1)}, bf16[512,128]{1,0:T(8,128)(2,1)S(1)}, u32[]{:S(2)}, u32[]{:S(2)}) collective-permute-start(bf16[512,128]{1,0:T(8,128)(2,1)S(1)} %stage.1.kv_ref), channel_id=1, source_target_pairs={{0,3},{1,4},{2,5},{3,6},{4,7},{5,8},{6,9},{7,10},{8,11},{9,12},{10... | collective-permute-start | bytes 393224 | tf_op jit(solution)/shard_map/ppermute | solution.py:277
  9.5 0.0 collective-permute-start
  9.5 2.9 %local.1 = (bf16[8,256,128]{2,1,0:T(8,128)(2,1)S(1)}, bf16[8,256,128]{2,1,0:T(8,128)(2,1)S(1)}, bf16[8,128,256]{2,1,0:T(8,128)(2,1)S(1)}, s32[1,256]{1,0:T(1,128...) custom-call(s32[1,128]{1,0:T(1,128)} %bitcast.1, ...), custom_call_target="tpu_custom_call" | custom-call | flops 402653184 | bytes 1180160 | tf_op jit(solution)/shard_map/local/pallas_call | solution.py:211
  12.4 0.0 collective-permute-done.3.kv_ref
  12.4 0.9 %score.7 = (f32[8,256,256]{2,1,0:T(8,128)S(1)}, f32[8,256,256]{2,1,0:T(8,128)S(1)}, f32[8,8,256]{2,1,0:T(8,128)S(1)}, bf16[128,256]{1,0:T(8,128)(2,1)S(1)}, bf16[136,256]{1,0:T(8,128)(2,1)S(1)}) custom-call(bf16[8,256,128]{2,1,0:T(8,128)(2,1)S(1)} %get-tuple-element.46.q_ref.refs_0_, bf16[8,256,128]{2,1,0:T(8,128)(2,1)S(1)} %get-tuple-element.47.do_ref.refs_1_, ...), custom_call_target="tpu_custom_call" | custom-call | flops 268435456 | bytes 1180672 | tf_op jit(solution)/shard_map/score/pallas_call | solution.py:211
  13.3 0.0 collective-permute-done.2.kv_ref
  13.3 0.2 score.6
  13.5 0.0 collective-permute-done.1.kv_ref
  13.6 0.2 score.5
  13.8 0.0 collective-permute-done.kv_ref
  13.8 0.2 score.4
  14.0 2.4 %remote.1 = (bf16[512,128]{1,0:T(8,128)(2,1)S(1)}, bf16[512,128]{1,0:T(8,128)(2,1)S(1)}, bf16[512,128]{1,0:T(8,128)(2,1)S(1)}, bf16[512,128]{1,0:T(8,128)(2,1)S(...) custom-call(s32[1,256]{1,0:T(1,128)S(1)} %get-tuple-element.45.begin, ...), custom_call_target="tpu_custom_call" | custom-call | flops 1610612736 | bytes 19956736 | tf_op jit(solution)/shard_map/remote/pallas_call | solution.py:211
  16.4 7.1 %collective-permute-start.4 = (bf16[512,128]{1,0:T(8,128)(2,1)S(1)}, bf16[512,128]{1,0:T(8,128)(2,1)S(1)}, u32[]{:S(2)}, u32[]{:S(2)}) collective-permute-start(bf16[512,128]{1,0:T(8,128)(2,1)S(1)} %get-tuple-element.82), channel_id=1, source_target_pairs={{0,255},{1,0},{2,1},{3,2},{4,3},{5,4},{6,5},{7,6},{8,7},{9,8},{10,... | collective-permute-start | bytes 393224 | tf_op jit(solution)/shard_map/ppermute | solution.py:277
  23.5 1.9 %collective-permute-start.5 = (bf16[512,128]{1,0:T(8,128)(2,1)S(1)}, bf16[512,128]{1,0:T(8,128)(2,1)S(1)}, u32[]{:S(2)}, u32[]{:S(2)}) collective-permute-start(bf16[512,128]{1,0:T(8,128)(2,1)S(1)} %get-tuple-element.83), channel_id=1, source_target_pairs={{0,254},{1,255},{2,0},{3,1},{4,2},{5,3},{6,4},{7,5},{8,6},{9,7},{1... | collective-permute-start | bytes 393224 | tf_op jit(solution)/shard_map/ppermute | solution.py:277
  25.3 3.3 %collective-permute-start.6 = (bf16[512,128]{1,0:T(8,128)(2,1)S(1)}, bf16[512,128]{1,0:T(8,128)(2,1)S(1)}, u32[]{:S(2)}, u32[]{:S(2)}) collective-permute-start(bf16[512,128]{1,0:T(8,128)(2,1)S(1)} %get-tuple-element.84), channel_id=1, source_target_pairs={{0,253},{1,254},{2,255},{3,0},{4,1},{5,2},{6,3},{7,4},{8,5},{9,6},... | collective-permute-start | bytes 393224 | tf_op jit(solution)/shard_map/ppermute | solution.py:277
  28.7 0.0 collective-permute-start.7
  28.7 2.6 %own.1 = (bf16[256,1024]{1,0:T(8,128)(2,1)}, bf16[256,1024]{1,0:T(8,128)(2,1)}, f32[512,128]{1,0:T(8,128)S(1)}) custom-call(bf16[8,256,128]{2,1,0:T(8,128)(2,1)S(1)} %get-tuple-element.68.q_low, bf16[8,256,128]{2,1,0:T(8,128)(2,1)S(1)} %get-tuple-element.69.do_low, f32[8,256,256]{2,1,0:T(8,128)S(1)} %get-tuple-element.70.s_own, ...), custom_call_target="tpu_custom_call" | custom-call | flops 939524096 | bytes 10903552 | tf_op jit(solution)/shard_map/own/pallas_call | solution.py:211
  31.3 0.0 collective-permute-done.4
  31.3 0.0 collective-permute-done.5
  31.3 0.0 collective-permute-done.6
  31.3 2.1 %collective-permute-done.7 = bf16[512,128]{1,0:T(8,128)(2,1)S(1)} collective-permute-done((bf16[512,128]{1,0:T(8,128)(2,1)S(1)}, bf16[512,128]{1,0:T(8,128)(2,1)S(1)}, u32[]{:S(2)}, u32[]{:S(2)}) %collective-permute-start.7) | collective-permute-done | bytes 131104 | tf_op jit(solution)/shard_map/ppermute | solution.py:277
  33.4 0.1 add_convert_fusion
  33.5 0.7 %fusion = (bf16[256,128]{1,0:T(8,128)(2,1)}, bf16[256,128]{1,0:T(8,128)(2,1)}) fusion(bf16[512,128]{1,0:T(8,128)(2,1)S(1)} %add_convert_fusion), kind=kLoop, calls=%fused_computation.1 | loop fusion | bytes 262144 | tf_op jit(solution)/shard_map/slice | solution.py:296
Async XLA Ops:
  1.5 10.8 %collective-permute-start.3 = (bf16[512,128]{1,0:T(8,128)(2,1)S(1)}, bf16[512,128]{1,0:T(8,128)(2,1)S(1)}, u32[]{:S(2)}, u32[]{:S(2)}) collective-permute-start(bf16[512,128]{1,0:T(8,128)(2,1)S(1)} %stage.1.kv_ref), channel_id=1, source_target_pairs={{0,1},{1,2},{2,3},{3,4},{4,5},{5,6},{6,7},{7,8},{8,9},{9,10},{10,1... | collective-permute-start | bytes 393224 | tf_op jit(solution)/shard_map/ppermute | solution.py:277
  3.7 9.7 %collective-permute-start.2 = (bf16[512,128]{1,0:T(8,128)(2,1)S(1)}, bf16[512,128]{1,0:T(8,128)(2,1)S(1)}, u32[]{:S(2)}, u32[]{:S(2)}) collective-permute-start(bf16[512,128]{1,0:T(8,128)(2,1)S(1)} %stage.1.kv_ref), channel_id=1, source_target_pairs={{0,2},{1,3},{2,4},{3,5},{4,6},{5,7},{6,8},{7,9},{8,10},{9,11},{10,... | collective-permute-start | bytes 393224 | tf_op jit(solution)/shard_map/ppermute | solution.py:277
  6.1 7.4 %collective-permute-start.1 = (bf16[512,128]{1,0:T(8,128)(2,1)S(1)}, bf16[512,128]{1,0:T(8,128)(2,1)S(1)}, u32[]{:S(2)}, u32[]{:S(2)}) collective-permute-start(bf16[512,128]{1,0:T(8,128)(2,1)S(1)} %stage.1.kv_ref), channel_id=1, source_target_pairs={{0,3},{1,4},{2,5},{3,6},{4,7},{5,8},{6,9},{7,10},{8,11},{9,12},{10... | collective-permute-start | bytes 393224 | tf_op jit(solution)/shard_map/ppermute | solution.py:277
  9.5 4.3 %collective-permute-start = (bf16[512,128]{1,0:T(8,128)(2,1)S(1)}, bf16[512,128]{1,0:T(8,128)(2,1)S(1)}, u32[]{:S(2)}, u32[]{:S(2)}) collective-permute-start(bf16[512,128]{1,0:T(8,128)(2,1)S(1)} %stage.1.kv_ref), channel_id=1, source_target_pairs={{0,4},{1,5},{2,6},{3,7},{4,8},{5,9},{6,10},{7,11},{8,12},{9,13},{1... | collective-permute-start | bytes 393224 | tf_op jit(solution)/shard_map/ppermute | solution.py:277
  16.4 14.9 %collective-permute-start.4 = (bf16[512,128]{1,0:T(8,128)(2,1)S(1)}, bf16[512,128]{1,0:T(8,128)(2,1)S(1)}, u32[]{:S(2)}, u32[]{:S(2)}) collective-permute-start(bf16[512,128]{1,0:T(8,128)(2,1)S(1)} %get-tuple-element.82), channel_id=1, source_target_pairs={{0,255},{1,0},{2,1},{3,2},{4,3},{5,4},{6,5},{7,6},{8,7},{9,8},{10,... | collective-permute-start | bytes 393224 | tf_op jit(solution)/shard_map/ppermute | solution.py:277
  23.5 7.9 %collective-permute-start.5 = (bf16[512,128]{1,0:T(8,128)(2,1)S(1)}, bf16[512,128]{1,0:T(8,128)(2,1)S(1)}, u32[]{:S(2)}, u32[]{:S(2)}) collective-permute-start(bf16[512,128]{1,0:T(8,128)(2,1)S(1)} %get-tuple-element.83), channel_id=1, source_target_pairs={{0,254},{1,255},{2,0},{3,1},{4,2},{5,3},{6,4},{7,5},{8,6},{9,7},{1... | collective-permute-start | bytes 393224 | tf_op jit(solution)/shard_map/ppermute | solution.py:277
  25.3 6.0 %collective-permute-start.6 = (bf16[512,128]{1,0:T(8,128)(2,1)S(1)}, bf16[512,128]{1,0:T(8,128)(2,1)S(1)}, u32[]{:S(2)}, u32[]{:S(2)}) collective-permute-start(bf16[512,128]{1,0:T(8,128)(2,1)S(1)} %get-tuple-element.84), channel_id=1, source_target_pairs={{0,253},{1,254},{2,255},{3,0},{4,1},{5,2},{6,3},{7,4},{8,5},{9,6},... | collective-permute-start | bytes 393224 | tf_op jit(solution)/shard_map/ppermute | solution.py:277
  28.7 4.7 %collective-permute-start.7 = (bf16[512,128]{1,0:T(8,128)(2,1)S(1)}, bf16[512,128]{1,0:T(8,128)(2,1)S(1)}, u32[]{:S(2)}, u32[]{:S(2)}) collective-permute-start(bf16[512,128]{1,0:T(8,128)(2,1)S(1)} %get-tuple-element.85), channel_id=1, source_target_pairs={{0,252},{1,253},{2,254},{3,255},{4,0},{5,1},{6,2},{7,3},{8,4},{9,5... | collective-permute-start | bytes 393224 | tf_op jit(solution)/shard_map/ppermute | solution.py:277
